TPU v7x, 256 devices: a whole 4x4x8 slice. The times are simulated.
256 devices in a mesh: dp: 32 (over x, z_hi, core), tensor: 8 (over y, z_lo).
Axes of the slice: x: 4, y: 4, z: 8 (z_hi: 4, z_lo: 2; z = z_hi * 2 + z_lo), core: 2. Of those that a mesh axis runs over, the one named last changes fastest.
Arguments:
- tokens: bfloat16 [1280, 4096], P(('dp', 'tensor')), may hold values from -6 to 6
- cotangent: bfloat16 [1280, 4096], P(('dp', 'tensor')), may hold values from -6 to 6
- gate_weight: bfloat16 [4096, 16384], P('tensor', 'dp'), may hold values from -0.09375 to 0.09375
- up_weight: bfloat16 [4096, 16384], P('tensor', 'dp'), may hold values from -0.09375 to 0.09375
- down_weight: bfloat16 [16384, 4096], P('dp', 'tensor'), may hold values from -0.046875 to 0.046875
- probe_gate: bfloat16 [4096, 16384], P('tensor', 'dp'), may hold values from -6 to 6
- probe_up: bfloat16 [4096, 16384], P('tensor', 'dp'), may hold values from -6 to 6
- probe_down: bfloat16 [16384, 4096], P('dp', 'tensor'), may hold values from -6 to 6
- hess_gate: float32 [4096, 16384], P('tensor', 'dp'), may hold values from 0.05 to 2
- hess_up: float32 [4096, 16384], P('tensor', 'dp'), may hold values from 0.05 to 2
- hess_down: float32 [16384, 4096], P('dp', 'tensor'), may hold values from 0.05 to 2
- moment_gate: bfloat16 [4096, 16384], P('tensor', 'dp'), may hold values from -0.125 to 0.125
- moment_up: bfloat16 [4096, 16384], P('tensor', 'dp'), may hold values from -0.125 to 0.125
- moment_down: bfloat16 [16384, 4096], P('dp', 'tensor'), may hold values from -0.125 to 0.125
Outputs:
- new_hess_gate: float32 [4096, 16384], P('tensor', 'dp')
- new_hess_up: float32 [4096, 16384], P('tensor', 'dp')
- new_hess_down: float32 [16384, 4096], P('dp', 'tensor')
- step_gate: bfloat16 [4096, 16384], P('tensor', 'dp')
- step_up: bfloat16 [4096, 16384], P('tensor', 'dp')
- step_down: bfloat16 [16384, 4096], P('dp', 'tensor')
All inputs are finite; a program needn't handle non-finite values.
Results may differ from a plain program's by a relative error of at most 0.0095.
Values may be sent and summed in bfloat16 or wider, within the bound.
A program may use at most 128 MiB of HBM per device.

v0:
```python
import jax
import jax.numpy as jnp
from jax import lax
from jax.sharding import PartitionSpec as P

decay_rate = 0.9
curvature_scale = 0.05
floor_value = 0.01


def contract_rows(former, latter):
    return lax.dot_general(
        former, latter, (((0,), (0,)), ((), ())), preferred_element_type=jnp.float32
    )


def contract_cols(former, latter):
    return lax.dot_general(
        former, latter, (((1,), (1,)), ((), ())), preferred_element_type=jnp.float32
    )


def tangent_terms(gate_pre, up_pre, back, gate_tan, up_tan, back_tan):
    logistic = jax.nn.sigmoid(gate_pre)
    activation = gate_pre * logistic
    first_deriv = logistic * (1.0 + gate_pre * (1.0 - logistic))
    second_deriv = logistic * (1.0 - logistic) * (2.0 + gate_pre * (1.0 - 2.0 * logistic))
    tan_gate_back = (
        back_tan * up_pre * first_deriv
        + back * up_tan * first_deriv
        + back * up_pre * second_deriv * gate_tan
    )
    tan_up_back = back_tan * activation + back * first_deriv * gate_tan
    tan_hidden = first_deriv * gate_tan * up_pre + activation * up_tan
    return (
        tan_gate_back.astype(jnp.bfloat16),
        tan_up_back.astype(jnp.bfloat16),
        tan_hidden.astype(jnp.bfloat16),
    )


def sophia_update(hess_prev, probe, product, moment):
    new_hess = decay_rate * hess_prev + (1.0 - decay_rate) * probe.astype(jnp.float32) * product
    ratio = moment.astype(jnp.float32) / jnp.maximum(curvature_scale * new_hess, floor_value)
    return (new_hess, jnp.clip(ratio, -1.0, 1.0).astype(jnp.bfloat16))


def local(
    tokens,
    cotangent,
    gate_weight,
    up_weight,
    down_weight,
    probe_gate,
    probe_up,
    probe_down,
    hess_gate,
    hess_up,
    hess_down,
    moment_gate,
    moment_up,
    moment_down,
):
    feature_width = gate_weight.shape[0]
    all_tokens, all_cotangent = (
        lax.all_gather(tokens, ("dp", "tensor"), axis=0, tiled=True),
        lax.all_gather(cotangent, ("dp", "tensor"), axis=0, tiled=True),
    )
    offset = lax.axis_index("tensor") * feature_width
    own_tokens = lax.dynamic_slice_in_dim(all_tokens, offset, feature_width, 1)
    own_cotangent = lax.dynamic_slice_in_dim(all_cotangent, offset, feature_width, 1)
    partials = (
        jnp.dot(own_tokens, gate_weight, preferred_element_type=jnp.float32),
        jnp.dot(own_tokens, up_weight, preferred_element_type=jnp.float32),
        contract_cols(own_cotangent, down_weight),
        jnp.dot(own_tokens, probe_gate, preferred_element_type=jnp.float32),
        jnp.dot(own_tokens, probe_up, preferred_element_type=jnp.float32),
        contract_cols(own_cotangent, probe_down),
    )
    summed = (
        lax.psum(partials[0].astype(jnp.bfloat16), "tensor").astype(jnp.float32),
        lax.psum(partials[1].astype(jnp.bfloat16), "tensor").astype(jnp.float32),
        lax.psum(partials[2].astype(jnp.bfloat16), "tensor").astype(jnp.float32),
        lax.psum(partials[3].astype(jnp.bfloat16), "tensor").astype(jnp.float32),
        lax.psum(partials[4].astype(jnp.bfloat16), "tensor").astype(jnp.float32),
        lax.psum(partials[5].astype(jnp.bfloat16), "tensor").astype(jnp.float32),
    )
    tan_gate_back, tan_up_back, tan_hidden = tangent_terms(
        summed[0], summed[1], summed[2], summed[3], summed[4], summed[5]
    )
    token_count = own_tokens.shape[0]
    product_gate = contract_rows(own_tokens, tan_gate_back) / token_count
    product_up = contract_rows(own_tokens, tan_up_back) / token_count
    product_down = contract_rows(tan_hidden, own_cotangent) / token_count
    new_hess_gate, step_gate = sophia_update(hess_gate, probe_gate, product_gate, moment_gate)
    new_hess_up, step_up = sophia_update(hess_up, probe_up, product_up, moment_up)
    new_hess_down, step_down = sophia_update(hess_down, probe_down, product_down, moment_down)
    return (new_hess_gate, new_hess_up, new_hess_down, step_gate, step_up, step_down)


def solution(mesh):
    return jax.shard_map(
        local,
        mesh=mesh,
        in_specs=(
            P(("dp", "tensor"), None),
            P(("dp", "tensor"), None),
            P("tensor", "dp"),
            P("tensor", "dp"),
            P("dp", "tensor"),
            P("tensor", "dp"),
            P("tensor", "dp"),
            P("dp", "tensor"),
            P("tensor", "dp"),
            P("tensor", "dp"),
            P("dp", "tensor"),
            P("tensor", "dp"),
            P("tensor", "dp"),
            P("dp", "tensor"),
        ),
        out_specs=(
            P("tensor", "dp"),
            P("tensor", "dp"),
            P("dp", "tensor"),
            P("tensor", "dp"),
            P("tensor", "dp"),
            P("dp", "tensor"),
        ),
        check_vma=False,
    )
```

profile of v0, /device:TPU:1, one launch (start us, length us, event | category | flops | bytes accessed | tf_op | source)
XLA Modules:
  0.0 1859.8 jit_solution(1563564398131186352)
XLA Ops:
  7.2 0.0 copy-start
  7.2 0.0 all-gather.7.cloned.1.call-start
  7.2 0.7 all-gather.7.cloned.1.call-update
  7.9 0.0 all-gather.5.cloned.1.call-start
  8.0 0.7 all-gather.5.cloned.1.call-update
  8.7 0.0 all-reduce.3.cloned.1.call-start
  8.7 736.3 %all-gather.7.cloned.1.call-done = bf16[256,5,4096]{2,1,0:T(8,128)(2,1)} async-done(((bf16[1,5,4096]{2,1,0:T(8,128)(2,1)}), bf16[256,5,4096]{2,1,0:T(8,128)(2,1)}) %all-gather.7.cloned.1.call-update) | async-done | bytes 10485776 | tf_op jit(solution)/shard_map/all_gather | solution.py:67
  745.0 16.8 reshape.15
  761.8 0.0 copy-done
  761.8 3.4 convolution_convert_fusion.3
  765.2 0.0 copy-done.13
  765.2 3.3 convolution_convert_fusion.5
  768.5 709.2 %all-gather.5.cloned.1.call-done = bf16[256,5,4096]{2,1,0:T(8,128)(2,1)} async-done(((bf16[1,5,4096]{2,1,0:T(8,128)(2,1)}), bf16[256,5,4096]{2,1,0:T(8,128)(2,1)}) %all-gather.5.cloned.1.call-update) | async-done | bytes 10485776 | tf_op jit(solution)/shard_map/all_gather | solution.py:66
  1477.7 16.9 reshape.13
  1494.6 0.0 copy-done.11
  1494.6 3.3 convolution_convert_fusion.1
  1497.9 3.3 convolution_convert_fusion.2
  1501.2 3.4 convolution_convert_fusion
  1504.5 0.0 copy-done.12
  1504.6 3.2 convolution_convert_fusion.4
  1507.8 0.0 all-reduce.3.cloned.1.call-update
  1507.8 328.2 %all-reduce.3.cloned.1.call-done = (bf16[1280,512]{1,0:T(8,128)(2,1)}, bf16[1280,512]{1,0:T(8,128)(2,1)}, bf16[1280,512]{1,0:T(8,128)(2,1)}, bf16[1280,512]{1,0:...) async-done(((bf16[1280,512]{1,0:T(8,128)(2,1)}, bf16[1280,512]{1,0:T(8,128)(2,1)}, bf16[1280,512]{1,0:T(8,128)(2,1)}, bf16[1280,512]{1,0:T(8,128)(2,1)}, ...) | async-done | bytes 7864336 | tf_op jit(solution)/shard_map/psum | solution.py:82
  1836.0 0.0 copy-done.8
  1836.0 0.0 copy-start.9
  1836.0 0.0 copy-start.15
  1836.0 6.5 clamp_convert_fusion
  1842.6 0.0 copy-done.3
  1842.6 0.0 copy-start.10
  1842.7 0.0 copy-start.18
  1842.7 5.6 clamp_convert_fusion.2
  1848.3 0.0 copy-done.18
  1848.3 5.0 clamp_convert_fusion.1
  (26 shorter events, 0.0 us)
Async XLA Ops:
  7.2 754.6 %copy-start = (bf16[512,512]{1,0:T(8,128)(2,1)S(1)}, bf16[512,512]{1,0:T(8,128)(2,1)}, u32[]{:S(2)}) copy-start(bf16[512,512]{1,0:T(8,128)(2,1)} %param.18) | copy-start | bytes 1572868
  7.2 737.8 %all-gather.7.cloned.1.call-start = ((), (), s32[]{:S(2)}) async-start(), calls=%async_computation.1 | async-start | bytes 16842752 | tf_op jit(solution)/shard_map/all_gather | solution.py:67
  7.9 1469.8 %all-gather.5.cloned.1.call-start = ((), (), s32[]{:S(2)}) async-start(), calls=%async_computation | async-start | bytes 16842752 | tf_op jit(solution)/shard_map/all_gather | solution.py:66
  8.7 1827.3 %all-reduce.3.cloned.1.call-start = ((), (), s32[]{:S(2)}) async-start(), calls=%async_computation.2 | async-start | bytes 15728640 | tf_op jit(solution)/shard_map/psum | solution.py:82
  761.8 3.4 copy-start.13
  768.5 726.1 %copy-start.11 = (bf16[512,512]{1,0:T(8,128)(2,1)S(1)}, bf16[512,512]{1,0:T(8,128)(2,1)}, u32[]{:S(2)}) copy-start(bf16[512,512]{1,0:T(8,128)(2,1)} %param.16) | copy-start | bytes 1572868
  1494.6 3.3 copy-start.17
  1497.9 3.3 copy-start.16
  1501.2 3.4 copy-start.12
  1507.8 328.2 %copy-start.8 = (f32[512,512]{1,0:T(8,128)S(1)}, f32[512,512]{1,0:T(8,128)}, u32[]{:S(2)}) copy-start(f32[512,512]{1,0:T(8,128)} %param.24) | copy-start | bytes 3145732
  1507.8 328.2 %copy-start.14 = (bf16[512,512]{1,0:T(8,128)(2,1)S(1)}, bf16[512,512]{1,0:T(8,128)(2,1)}, u32[]{:S(2)}) copy-start(bf16[512,512]{1,0:T(8,128)(2,1)} %param.27) | copy-start | bytes 1572868
  1836.0 6.6 copy-start.2
  1836.0 6.6 copy-start.3
  1836.0 6.6 copy-start.4
  1836.0 6.6 copy-start.5
  1836.0 6.6 copy-start.6
  1836.0 6.6 copy-start.7
  1836.0 6.6 copy-start.9
  1836.0 6.6 copy-start.15
  1842.6 5.6 copy-start.10
  1842.7 5.6 copy-start.18
  1848.3 5.0 copy-start.1
Sparse Core Ops, SparseCore 0:
  9.9 735.0 all-gather.6
  746.8 730.8 all-gather.4
  1507.9 327.9 all-reduce.2
where the time goes:
time: 1860 us
  waiting for transfers between devices  1780 us (96%)
  matrix products  37 us (2%)
  local copies, waits for them, and re-layouts  33.8 us (2%)
    all_gather x1, waiting for transfers between devices, local(): lax.all_gather(cotangent, ('dp', 'tensor'), axis=0, tiled=True)  736 us
    all_gather x1, waiting for transfers between devices, local(): lax.all_gather(tokens, ('dp', 'tensor'), axis=0, tiled=True)  709 us
    psum x1, waiting for transfers between devices, local(): lax.psum(partials[1].astype(jnp.bfloat16), 'tensor').astype(jnp.float32)  328 us
  transfers between devices with their start and end apart: 3, of which 3 were waited for; matrix products, arithmetic and copies ran while one was open for 1% of the time, Pallas kernels for 0%

commit v1 on v0

v1 whole, which is shorter than its diff:
```python
import jax
import jax.numpy as jnp
import numpy as np
from jax import lax
from jax.experimental import pallas as pl
from jax.experimental.pallas import tpu as pltpu
from jax.sharding import PartitionSpec as P

decay_rate = 0.9
curvature_scale = 0.05
floor_value = 0.01

MESH = pl.DeviceIdType.MESH
ANY = pl.BlockSpec(memory_space=pl.ANY)
VMEM = pl.BlockSpec(memory_space=pltpu.VMEM)
DMA = pltpu.SemaphoreType.DMA

NX, NY, NZ = 4, 4, 4
ROWS = 5
GROUP = 80
FEAT = 512
WIDE = NY * FEAT
TOKENS = 1280
SUB = 128


def place():
    d = lax.axis_index("dp")
    t = lax.axis_index("tensor")
    return d // 8, t // 2, (d // 2) % 4, t % 2, d % 2


def device(x, y, zh, zl, c):
    return {"dp": x * 8 + zh * 2 + c, "tensor": y * 2 + zl}


def remote(src, dst, send, recv, target):
    return pltpu.make_async_remote_copy(
        src_ref=src, dst_ref=dst, send_sem=send, recv_sem=recv,
        device_id=target, device_id_type=MESH,
    )


def enter(targets):
    barrier = pltpu.get_barrier_semaphore()
    for target in targets:
        pl.semaphore_signal(barrier, inc=1, device_id=target, device_id_type=MESH)
    pl.semaphore_wait(barrier, len(targets))


def gather_kernel(
    tok_ref, cot_ref, pick_ref, gate_ref, up_ref, pgate_ref, pup_ref, down_ref, pdown_ref,
    all_ref, wide_ref, tall_ref,
    packed32, packed, pieces, block,
    ps, pr, ws, wr, wl, zs, zr, xs, xr, ss, sr, own_sem,
):
    x, y, zh, zl, c = place()
    group = [(dc, dy, dz) for dc in range(2) for dy in range(4) for dz in range(2)][1:]
    mates = [((y + dy) % 4, zl ^ dz, c ^ dc) for dc, dy, dz in group]
    sib = device(x, y, zh, zl, 1 - c)
    zn, zp = device(x, y, (zh + 1) % 4, zl, c), device(x, y, (zh + 3) % 4, zl, c)
    xn, xp = device((x + 1) % 4, y, zh, zl, c), device((x + 3) % 4, y, zh, zl, c)
    enter([device(x, my, zh, mz, mc) for my, mz, mc in mates] + [zn, zp, xn, xp])

    for arr, ref in enumerate((tok_ref, cot_ref)):
        for mz in range(2):
            packed32[...] = jnp.zeros_like(packed32)
            for my in range(4):
                col = (my * 2 + mz) * FEAT
                packed32[8 * (my // 2):8 * (my // 2) + ROWS, (my % 2) * FEAT:(my % 2 + 1) * FEAT] = (
                    ref[:, col:col + FEAT].astype(jnp.float32)
                )
            packed[mz, arr] = packed32[...].astype(jnp.bfloat16)
    me = c * 8 + y * 2 + zl
    piece_copies = []
    for k, (my, mz, mc) in enumerate(mates):
        cp = remote(packed.at[mz, mc], pieces.at[me], ps.at[k], pr.at[k], device(x, my, zh, mz, mc))
        cp.start()
        piece_copies.append(cp)
    pieces[me] = packed[zl, c]

    weight_copies = []
    col_refs = (gate_ref, up_ref, pgate_ref, pup_ref)
    row_refs = (down_ref, pdown_ref)

    def cut(k, to):
        if k < 4:
            return (
                col_refs[k].at[:, pl.ds(pl.multiple_of(to * SUB, SUB), SUB)],
                wide_ref.at[pl.ds(pl.multiple_of(y * FEAT, FEAT), FEAT), pl.ds(k * SUB, SUB)],
            )
        return (
            row_refs[k - 4].at[pl.ds(pl.multiple_of(to * SUB, SUB), SUB), :],
            tall_ref.at[pl.ds((k - 4) * SUB, SUB), pl.ds(pl.multiple_of(y * FEAT, FEAT), FEAT)],
        )

    for k in range(6):
        for dy in (1, 3, 2):
            to = (y + dy) % 4
            src, dst = cut(k, to)
            cp = remote(src, dst, ws.at[dy - 1, k], wr.at[dy - 1, k], device(x, to, zh, zl, c))
            cp.start()
            weight_copies.append(cp)
        src, dst = cut(k, y)
        cp = pltpu.make_async_copy(src, dst, wl.at[k])
        cp.start()
        weight_copies.append(cp)

    for cp in piece_copies:
        cp.wait_recv()
    spread = pieces[...].reshape(256, 1024)
    for half in range(2):
        block[:, half * 1024:(half + 1) * 1024] = jnp.dot(
            pick_ref[half], spread, preferred_element_type=jnp.float32
        ).astype(jnp.bfloat16)

    HALF = WIDE // 2
    zrel = (0, 3, 1, 2)
    sends = []
    pending = {}

    def where(dx, k, half=None):
        g = ((x + dx) % 4) * 4 + (zh + zrel[k]) % 4
        rows = pl.ds(pl.multiple_of(g * GROUP, 16), GROUP)
        if half is None:
            return all_ref.at[c, rows, :]
        return all_ref.at[c, rows, pl.ds(half * HALF, HALF)]

    def go(src, dst, s, r, target):
        cp = remote(src, dst, s, r, target)
        cp.start()
        sends.append(cp)

    def arrive(dst, s, r):
        remote(dst, dst, s, r, sib).wait_recv()

    def share(dx, k, src=None):
        ref = where(dx, k)
        n = dx * 4 + k
        go(ref if src is None else src, ref, ss.at[n], sr.at[n], sib)

    def along_x(k, src=None):
        ref = where(0, k)
        src = ref if src is None else src
        go(src, ref, xs.at[0, k], xr.at[0, k], xn)
        go(src, ref, xs.at[1, k], xr.at[1, k], xp)

    def pass_x(k):
        arrive(where(3, k), xs.at[0, k], xr.at[0, k])
        half = where(3, k, 0)
        go(half, half, xs.at[2, k], xr.at[2, k], xn)
        arrive(where(1, k), xs.at[1, k], xr.at[1, k])
        half = where(1, k, 1)
        go(half, half, xs.at[3, k], xr.at[3, k], xp)
        share(3, k)
        share(1, k)

    def end_x(k):
        arrive(where(2, k, 0), xs.at[2, k], xr.at[2, k])
        arrive(where(2, k, 1), xs.at[3, k], xr.at[3, k])
        share(2, k)

    here = where(0, 0)
    go(block, here, zs.at[0], zr.at[0], zn)
    go(block, here, zs.at[1], zr.at[1], zp)
    along_x(0, block)
    share(0, 0, block)
    keep = pltpu.make_async_copy(block, here, own_sem)
    keep.start()
    pass_x(0)
    arrive(where(0, 1), zs.at[0], zr.at[0])
    half = where(0, 1, 0)
    go(half, half, zs.at[2], zr.at[2], zn)
    arrive(where(0, 2), zs.at[1], zr.at[1])
    half = where(0, 2, 1)
    go(half, half, zs.at[3], zr.at[3], zp)
    along_x(1)
    along_x(2)
    share(0, 1)
    share(0, 2)
    end_x(0)
    arrive(where(0, 3, 0), zs.at[2], zr.at[2])
    arrive(where(0, 3, 1), zs.at[3], zr.at[3])
    along_x(3)
    share(0, 3)
    pass_x(1)
    pass_x(2)
    end_x(1)
    end_x(2)
    pass_x(3)
    end_x(3)
    for cp in weight_copies:
        cp.wait()
    keep.wait()
    for cp in piece_copies:
        cp.wait_send()
    for cp in sends:
        cp.wait_send()
    for dx in range(4):
        for k in range(4):
            g = ((x + dx) % 4) * 4 + (zh + zrel[k]) % 4
            ref = all_ref.at[1 - c, pl.ds(pl.multiple_of(g * GROUP, 16), GROUP), :]
            arrive(ref, ss.at[dx * 4 + k], sr.at[dx * 4 + k])


def gather(tokens, cotangent, gate, up, pgate, pup, down, pdown):
    pick = np.zeros((2, GROUP, 256), np.float32)
    for half in range(2):
        for row in range(GROUP):
            pick[half, row, 16 * (row // ROWS) + row % ROWS + 8 * half] = 1.0
    bf = jnp.bfloat16
    return pl.pallas_call(
        gather_kernel,
        out_shape=(
            jax.ShapeDtypeStruct((2, TOKENS, WIDE), bf),
            jax.ShapeDtypeStruct((WIDE, 4 * SUB), bf),
            jax.ShapeDtypeStruct((2 * SUB, WIDE), bf),
        ),
        in_specs=[VMEM] * 3 + [ANY] * 6,
        out_specs=(ANY, ANY, ANY),
        scratch_shapes=[
            pltpu.VMEM((16, 1024), jnp.float32),
            pltpu.VMEM((2, 2, 16, 1024), bf),
            pltpu.VMEM((16, 16, 1024), bf),
            pltpu.VMEM((GROUP, WIDE), bf),
            DMA((15,)), DMA((15,)),
            DMA((3, 6)), DMA((3, 6)), DMA((6,)),
            DMA((4,)), DMA((4,)),
            DMA((4, 4)), DMA((4, 4)),
            DMA((16,)), DMA((16,)),
            DMA(()),
        ],
        compiler_params=pltpu.CompilerParams(
            collective_id=0, has_side_effects=True, vmem_limit_bytes=40 << 20
        ),
    )(tokens, cotangent, jnp.asarray(pick, bf), gate, up, pgate, pup, down, pdown)


CHUNKS = 4
CHUNK = TOKENS // 2 // CHUNKS


def tangent_kernel(sums_ref, back_ref, out_ref, far_sums, far_back, s1, r1, s2, r2, s3, r3):
    x, y, zh, zl, c = place()
    mate = device(x, y, zh, 1 - zl, c)
    enter([mate])
    copies = []
    for k in range(CHUNKS):
        rows = pl.ds(pl.multiple_of((1 - zl) * (TOKENS // 2) + k * CHUNK, 16), CHUNK)
        a = remote(sums_ref.at[rows, :], far_sums.at[k], s1.at[k], r1.at[k], mate)
        b = remote(back_ref.at[rows, :], far_back.at[k], s2.at[k], r2.at[k], mate)
        a.start()
        b.start()
        copies.append((a, b))
    outs = []
    for k in range(CHUNKS):
        for cp in copies[k]:
            cp.wait_recv()
        rows = pl.ds(pl.multiple_of(zl * (TOKENS // 2) + k * CHUNK, 16), CHUNK)

        def total(near, far, n):
            cols = slice(n * SUB, (n + 1) * SUB)
            return near[rows, cols].astype(jnp.float32) + far[k, :, cols].astype(jnp.float32)

        gate_pre, up_pre, gate_tan, up_tan = (total(sums_ref, far_sums, n) for n in range(4))
        back, back_tan = (total(back_ref, far_back, n) for n in range(2))
        logistic = 1.0 / (1.0 + jnp.exp(-gate_pre))
        activation = gate_pre * logistic
        first = logistic * (1.0 + gate_pre * (1.0 - logistic))
        second = logistic * (1.0 - logistic) * (2.0 + gate_pre * (1.0 - 2.0 * logistic))
        out_ref[rows, 0:SUB] = (
            back_tan * up_pre * first + back * up_tan * first + back * up_pre * second * gate_tan
        ).astype(jnp.bfloat16)
        out_ref[rows, SUB:2 * SUB] = (back_tan * activation + back * first * gate_tan).astype(jnp.bfloat16)
        out_ref[rows, 2 * SUB:] = (first * gate_tan * up_pre + activation * up_tan).astype(jnp.bfloat16)
        cp = remote(out_ref.at[rows, :], out_ref.at[rows, :], s3.at[k], r3.at[k], mate)
        cp.start()
        outs.append(cp)
    for k in range(CHUNKS):
        rows = pl.ds(pl.multiple_of((1 - zl) * (TOKENS // 2) + k * CHUNK, 16), CHUNK)
        remote(out_ref.at[rows, :], out_ref.at[rows, :], s3.at[k], r3.at[k], mate).wait_recv()
        for cp in copies[k]:
            cp.wait_send()
        outs[k].wait_send()


def tangents(sums, back):
    bf = jnp.bfloat16
    return pl.pallas_call(
        tangent_kernel,
        out_shape=jax.ShapeDtypeStruct((TOKENS, 3 * SUB), bf),
        in_specs=[VMEM] * 2,
        out_specs=VMEM,
        scratch_shapes=[
            pltpu.VMEM((CHUNKS, CHUNK, 4 * SUB), bf),
            pltpu.VMEM((CHUNKS, CHUNK, 2 * SUB), bf),
        ] + [DMA((CHUNKS,))] * 6,
        compiler_params=pltpu.CompilerParams(
            collective_id=1, has_side_effects=True, vmem_limit_bytes=40 << 20
        ),
    )(sums, back)


def return_kernel(wide_ref, tall_ref, gate_ref, up_ref, down_ref, send, recv, local_sem):
    x, y, zh, zl, c = place()
    enter([device(x, (y + dy) % 4, zh, zl, c) for dy in (1, 2, 3)])

    def cut(k, to):
        feats = pl.ds(pl.multiple_of(to * FEAT, FEAT), FEAT)
        mine = pl.ds(pl.multiple_of(y * SUB, SUB), SUB)
        if k < 2:
            return wide_ref.at[feats, pl.ds(k * SUB, SUB)], (gate_ref, up_ref)[k].at[:, mine]
        return tall_ref.at[:, feats], down_ref.at[mine, :]

    copies = []
    for k in range(3):
        for dy in (1, 3, 2):
            to = (y + dy) % 4
            src, dst = cut(k, to)
            cp = remote(src, dst, send.at[dy - 1, k], recv.at[dy - 1, k], device(x, to, zh, zl, c))
            cp.start()
            copies.append(cp)
        src, dst = cut(k, y)
        cp = pltpu.make_async_copy(src, dst, local_sem.at[k])
        cp.start()
        copies.append(cp)
    for cp in copies:
        cp.wait()


def give_back(wide, tall):
    bf = jnp.bfloat16
    return pl.pallas_call(
        return_kernel,
        out_shape=(jax.ShapeDtypeStruct((FEAT, 4 * SUB), bf),) * 2 + (jax.ShapeDtypeStruct((4 * SUB, FEAT), bf),),
        in_specs=[VMEM] * 2,
        out_specs=(VMEM,) * 3,
        scratch_shapes=[DMA((3, 3)), DMA((3, 3)), DMA((3,))],
        compiler_params=pltpu.CompilerParams(
            collective_id=2, has_side_effects=True, vmem_limit_bytes=40 << 20
        ),
    )(wide, tall)


def sophia_update(hess_prev, probe, product, moment):
    new_hess = decay_rate * hess_prev + (1.0 - decay_rate) * probe.astype(jnp.float32) * product.astype(jnp.float32)
    ratio = moment.astype(jnp.float32) / jnp.maximum(curvature_scale * new_hess, floor_value)
    return new_hess, jnp.clip(ratio, -1.0, 1.0).astype(jnp.bfloat16)


def local(
    tokens, cotangent, gate_weight, up_weight, down_weight, probe_gate, probe_up, probe_down,
    hess_gate, hess_up, hess_down, moment_gate, moment_up, moment_down,
):
    every, wide, tall = gather(
        tokens, cotangent, gate_weight, up_weight, probe_gate, probe_up, down_weight, probe_down
    )
    toks, cots = every[0], every[1]
    f32, bf = jnp.float32, jnp.bfloat16
    sums = jnp.dot(toks, wide, preferred_element_type=f32).astype(bf)
    back = lax.dot_general(cots, tall, (((1,), (1,)), ((), ())), preferred_element_type=f32).astype(bf)
    tans = tangents(sums, back)
    wide_out = lax.dot_general(toks, tans[:, :2 * SUB], (((0,), (0,)), ((), ())), preferred_element_type=f32)
    tall_out = lax.dot_general(tans[:, 2 * SUB:], cots, (((0,), (0,)), ((), ())), preferred_element_type=f32)
    products = give_back((wide_out / TOKENS).astype(bf), (tall_out / TOKENS).astype(bf))
    new_hess_gate, step_gate = sophia_update(hess_gate, probe_gate, products[0], moment_gate)
    new_hess_up, step_up = sophia_update(hess_up, probe_up, products[1], moment_up)
    new_hess_down, step_down = sophia_update(hess_down, probe_down, products[2], moment_down)
    return new_hess_gate, new_hess_up, new_hess_down, step_gate, step_up, step_down


def solution(mesh):
    cols, rows, split = P("tensor", "dp"), P("dp", "tensor"), P(("dp", "tensor"), None)
    per = (cols, cols, rows)
    return jax.shard_map(
        local, mesh=mesh,
        in_specs=(split, split) + per * 4,
        out_specs=per * 2,
        check_vma=False,
    )
```

time: 1860 us -> 153 us (0.08)
  waiting for transfers between devices: 1780 us -> 0 us
  Pallas kernels: 0 us -> 129 us
  matrix products: 37 us -> 9.6 us
  local copies, waits for them, and re-layouts: 33.8 us -> 10.2 us
    all_gather x2 -> x0, waiting for transfers between devices: 1450 us -> none  [the longest x1 736 us: local(): lax.all_gather(cotangent, ('dp', 'tensor'), axis=0, tiled=True)]
    psum x1 -> x0, waiting for transfers between devices: 328 us -> none  [local(): lax.psum(partials[1].astype(jnp.bfloat16), 'tensor').astype(jnp.float32)]
    pallas_call x0 -> x3, Pallas kernels: none -> 129 us  [the longest x1 73.7 us: gather(): pl.pallas_call(gather_kernel, out_shape=(jax.ShapeDtypeStruct((2, TOKENS,...]
    dot_general x9 -> x4, matrix products: 37 us -> 9.6 us  [the longest x1 4.21 us: local(): lax.dot_general(cots, tall, (((1,), (1,)), ((), ())), preferred_element_t...]
    unnamed x40 -> x38, local copies, waits for them, and re-layouts: 33.8 us -> 10.2 us
  transfers between devices with their start and end apart: 3 -> 0, of which waited for: 3 -> 0; matrix products, arithmetic and copies ran while one was open for 1% -> 0% of each run, Pallas kernels for 0% -> 0%
where the time goes in v1:
time: 153 us
  Pallas kernels  129 us (84%)
  local copies, waits for them, and re-layouts  10.2 us (7%)
  matrix products  9.6 us (6%)
  other arithmetic  3.66 us (2%)
    pallas_call x1, Pallas kernels, gather(): pl.pallas_call(gather_kernel, out_shape=(jax.ShapeDtypeStruct((2, TOKENS,...  73.7 us
    pallas_call x1, Pallas kernels, tangents(): pl.pallas_call(tangent_kernel, out_shape=jax.ShapeDtypeStruct((TOKENS, 3...  34.8 us
    pallas_call x1, Pallas kernels, give_back(): pl.pallas_call(return_kernel, out_shape=(jax.ShapeDtypeStruct((FEAT, 4 *...  20.2 us
    unnamed x38, local copies, waits for them, and re-layouts  10.2 us
    dot_general x1, matrix products, local(): lax.dot_general(cots, tall, (((1,), (1,)), ((), ())), preferred_element_t...  4.21 us
    convert_element_type x2, other arithmetic, sophia_update(): return (new_hess, jnp.clip(ratio, -1.0, 1.0).astype(jnp.bfloat16))  3.66 us

profile of v1, /device:TPU:1, one launch (start us, length us, event | category | flops | bytes accessed | tf_op | source)
XLA Modules:
  0.0 153.0 jit_solution(9785523016680691657)
XLA Ops:
  0.6 0.0 copy-start
  0.6 1.0 copy-done
  1.7 1.0 copy-done.2
  2.7 1.0 copy-done.4
  3.8 1.0 copy-done.6
  4.8 1.0 copy-done.7
  5.8 1.0 copy-done.8
  6.9 0.9 copy-done.9
  7.8 0.8 copy-done.10
  8.6 0.8 copy-done.11
  9.5 73.7 %shard_map.190 = (bf16[2,1280,2048]{2,1,0:T(8,128)(2,1)}, bf16[2048,512]{1,0:T(8,128)(2,1)S(1)}, bf16[256,2048]{1,0:T(8,128)(2,1)S(1)}) custom-call(bf16[5,4096]{1,0:T(8,128)(2,1)S(1)} %copy-done.10, bf16[5,4096]{1,0:T(8,128)(2,1)S(1)} %copy-done.11, bf16[2,80,256]{2,1,0:T(8,128)(2,1)S(1)} %copy-done.9, bf16[512,512]{1,0:T(8,128)(2,1)S(1)} %copy-done.6, ...), custom_call_target="tpu_custom_call" | custom-call | tf_op jit(solution)/shard_map/pallas_call | solution.py:212
  83.1 0.0 copy-start.18
  83.2 4.2 %fusion.21.back_ref = bf16[1280,256]{1,0:T(8,128)(2,1)S(1)} fusion(bf16[256,2048]{1,0:T(8,128)(2,1)S(1)} %get-tuple-element.14, bf16[2,1280,2048]{2,1,0:T(8,128)(2,1)} %get-tuple-element.12), kind=kOutput, calls=%fused_computation.15 | convolution fusion | flops 1342504960 | bytes 6946816 | tf_op jit(solution)/shard_map/dot_general | solution.py:361
  87.4 1.3 copy-done.18
  88.7 2.9 %fusion.12.sums_ref = bf16[1280,512]{1,0:T(8,128)(2,1)S(1)} fusion(bf16[2048,512]{1,0:T(8,128)(2,1)S(1)} %get-tuple-element.13, bf16[2,1280,2048]{2,1,0:T(8,128)(2,1)S(1)} %copy-done.18), kind=kOutput, calls=%fused_computation.12 | convolution fusion | flops 2685009920 | bytes 8650752 | tf_op jit(solution)/shard_map/dot_general | solution.py:360
  91.6 34.8 %shard_map.191 = bf16[1280,384]{1,0:T(8,128)(2,1)S(1)} custom-call(bf16[1280,512]{1,0:T(8,128)(2,1)S(1)} %fusion.12.sums_ref, bf16[1280,256]{1,0:T(8,128)(2,1)S(1)} %fusion.21.back_ref), custom_call_target="tpu_custom_call" | custom-call | tf_op jit(solution)/shard_map/pallas_call | solution.py:289
  126.4 0.9 fusion.27.tall_ref
  127.2 0.0 copy-start.1
  127.3 0.0 copy-start.3
  127.3 0.0 copy-start.13
  127.3 0.0 copy-start.14
  127.3 0.0 copy-start.15
  127.3 0.0 copy-start.16
  127.3 1.6 %fusion.18.wide_ref = bf16[2048,256]{1,0:T(8,128)(2,1)S(1)} fusion(bf16[2,1280,2048]{2,1,0:T(8,128)(2,1)S(1)} %copy-done.18, bf16[1280,384]{1,0:T(8,128)(2,1)S(1)} %shard_map.191), kind=kOutput, calls=%fused_computation.14 | convolution fusion | flops 1343225856 | bytes 6946816 | tf_op jit(solution)/shard_map/dot_general | solution.py:363
  129.0 0.0 copy-start.5
  129.0 0.0 copy-start.12
  129.0 0.0 copy-start.17
  129.0 20.2 %shard_map.192 = (bf16[512,512]{1,0:T(8,128)(2,1)S(1)}, bf16[512,512]{1,0:T(8,128)(2,1)S(1)}, bf16[512,512]{1,0:T(8,128)(2,1)S(1)}) custom-call(bf16[2048,256]{1,0:T(8,128)(2,1)S(1)} %fusion.18.wide_ref, bf16[128,2048]{1,0:T(8,128)(2,1)S(1)} %fusion.27.tall_ref), custom_call_target="tpu_custom_call" | custom-call | tf_op jit(solution)/shard_map/pallas_call | solution.py:333
  149.2 0.0 copy-done.1
  149.2 0.0 copy-done.3
  149.3 2.1 %clamp_convert_fusion = (bf16[512,512]{1,0:T(8,128)(2,1)}, f32[512,512]{1,0:T(8,128)}, bf16[512,512]{1,0:T(8,128)(2,1)}, f32[512,512]{1,0:T(8,128)}) fusion(bf16[512,512]{1,0:T(8,128)(2,1)S(1)} %copy-done.15, bf16[512,512]{1,0:T(8,128)(2,1)S(1)} %get-tuple-element.17, bf16[512,512]{1,0:T(8,128)(2,1)S(1)} %copy-done.3, f32[512,512]{1,0:T(8,128)S(1)} %copy-done.13, ...), kind=kLoop, calls=%fused_computation.18 | loop fusion | flops 6291456 | bytes 8388608 | tf_op jit(solution)/shard_map/convert_element_type | solution.py:348
  151.4 1.6 %clamp_convert_fusion.2 = (bf16[512,512]{1,0:T(8,128)(2,1)}, f32[512,512]{1,0:T(8,128)}) fusion(bf16[512,512]{1,0:T(8,128)(2,1)S(1)} %copy-done.17, bf16[512,512]{1,0:T(8,128)(2,1)S(1)} %get-tuple-element.15, bf16[512,512]{1,0:T(8,128)(2,1)S(1)} %copy-done.5, f32[512,512]{1,0:T(8,128)S(1)} %copy-done.12), kind=kLoop, calls=%fused_computation.20 | loop fusion | flops 3145728 | bytes 4194304 | tf_op jit(solution)/shard_map/convert_element_type | solution.py:348
  (15 shorter events, 0.0 us)
Async XLA Ops:
  0.6 1.0 copy-start
  1.7 1.0 copy-start.2
  2.7 1.0 copy-start.4
  3.8 1.0 copy-start.6
  4.8 1.0 copy-start.7
  5.8 1.0 copy-start.8
  6.9 0.9 copy-start.9
  7.8 0.8 copy-start.10
  8.6 0.8 copy-start.11
  83.1 5.5 %copy-start.18 = (bf16[2,1280,2048]{2,1,0:T(8,128)(2,1)S(1)}, bf16[2,1280,2048]{2,1,0:T(8,128)(2,1)}, u32[]{:S(2)}) copy-start(bf16[2,1280,2048]{2,1,0:T(8,128)(2,1)} %get-tuple-element.12) | copy-start | bytes 31457284
  127.2 22.0 %copy-start.1 = (bf16[512,512]{1,0:T(8,128)(2,1)S(1)}, bf16[512,512]{1,0:T(8,128)(2,1)}, u32[]{:S(2)}) copy-start(bf16[512,512]{1,0:T(8,128)(2,1)} %pup_ref.1) | copy-start | bytes 1572868
  127.3 22.0 %copy-start.3 = (bf16[512,512]{1,0:T(8,128)(2,1)S(1)}, bf16[512,512]{1,0:T(8,128)(2,1)}, u32[]{:S(2)}) copy-start(bf16[512,512]{1,0:T(8,128)(2,1)} %pdown_ref.1) | copy-start | bytes 1572868
  127.3 22.0 %copy-start.13 = (f32[512,512]{1,0:T(8,128)S(1)}, f32[512,512]{1,0:T(8,128)}, u32[]{:S(2)}) copy-start(f32[512,512]{1,0:T(8,128)} %param.25) | copy-start | bytes 3145732
  127.3 22.0 %copy-start.14 = (f32[512,512]{1,0:T(8,128)S(1)}, f32[512,512]{1,0:T(8,128)}, u32[]{:S(2)}) copy-start(f32[512,512]{1,0:T(8,128)} %param.24) | copy-start | bytes 3145732
  127.3 22.0 %copy-start.15 = (bf16[512,512]{1,0:T(8,128)(2,1)S(1)}, bf16[512,512]{1,0:T(8,128)(2,1)}, u32[]{:S(2)}) copy-start(bf16[512,512]{1,0:T(8,128)(2,1)} %param.28) | copy-start | bytes 1572868
  127.3 22.0 %copy-start.16 = (bf16[512,512]{1,0:T(8,128)(2,1)S(1)}, bf16[512,512]{1,0:T(8,128)(2,1)}, u32[]{:S(2)}) copy-start(bf16[512,512]{1,0:T(8,128)(2,1)} %param.27) | copy-start | bytes 1572868
  129.0 22.4 %copy-start.5 = (bf16[512,512]{1,0:T(8,128)(2,1)S(1)}, bf16[512,512]{1,0:T(8,128)(2,1)}, u32[]{:S(2)}) copy-start(bf16[512,512]{1,0:T(8,128)(2,1)} %pgate_ref.1) | copy-start | bytes 1572868
  129.0 22.4 %copy-start.12 = (f32[512,512]{1,0:T(8,128)S(1)}, f32[512,512]{1,0:T(8,128)}, u32[]{:S(2)}) copy-start(f32[512,512]{1,0:T(8,128)} %param.23) | copy-start | bytes 3145732
  129.0 22.4 %copy-start.17 = (bf16[512,512]{1,0:T(8,128)(2,1)S(1)}, bf16[512,512]{1,0:T(8,128)(2,1)}, u32[]{:S(2)}) copy-start(bf16[512,512]{1,0:T(8,128)(2,1)} %param.26) | copy-start | bytes 1572868

commit v2 on v1

v2 whole, which is shorter than its diff:
```python
import jax
import jax.numpy as jnp
import numpy as np
from jax import lax
from jax.experimental import pallas as pl
from jax.experimental.pallas import tpu as pltpu
from jax.sharding import PartitionSpec as P

decay_rate = 0.9
curvature_scale = 0.05
floor_value = 0.01

MESH = pl.DeviceIdType.MESH
ANY = pl.BlockSpec(memory_space=pl.ANY)
VMEM = pl.BlockSpec(memory_space=pltpu.VMEM)
DMA = pltpu.SemaphoreType.DMA

NX, NY, NZ = 4, 4, 4
ROWS = 5
GROUP = 80
FEAT = 512
WIDE = NY * FEAT
TOKENS = 1280
SUB = 128


def place():
    d = lax.axis_index("dp")
    t = lax.axis_index("tensor")
    return d // 8, t // 2, (d // 2) % 4, t % 2, d % 2


def device(x, y, zh, zl, c):
    return {"dp": x * 8 + zh * 2 + c, "tensor": y * 2 + zl}


def remote(src, dst, send, recv, target):
    return pltpu.make_async_remote_copy(
        src_ref=src, dst_ref=dst, send_sem=send, recv_sem=recv,
        device_id=target, device_id_type=MESH,
    )


def enter(targets):
    barrier = pltpu.get_barrier_semaphore()
    for target in targets:
        pl.semaphore_signal(barrier, inc=1, device_id=target, device_id_type=MESH)
    pl.semaphore_wait(barrier, len(targets))

HALF = WIDE // 2
SPAN = TOKENS // NX
OWN = SPAN // 2
ZREL = (0, 3, 1, 2)


def refresh_kernel(
    tok_ref, cot_ref, pick_ref, gate_ref, up_ref, pgate_ref, pup_ref, down_ref, pdown_ref,
    gate_out, up_out, down_out,
    packed32, packed, pieces, every, wide, tall, part, far, tans, back_wide, back_tall,
    ps, pr, ws, wr, wl, zs, zr, xs, xr, ss, sr, rs, rr, ts, tr, os, orr, ol,
):
    x, y, zh, zl, c = place()
    f32, bf = jnp.float32, jnp.bfloat16
    group = [(dc, dy, dz) for dc in range(2) for dy in range(4) for dz in range(2)][1:]
    mates = [((y + dy) % 4, zl ^ dz, c ^ dc) for dc, dy, dz in group]
    sib = device(x, y, zh, zl, 1 - c)
    pair = device(x, y, zh, 1 - zl, c)
    zn, zp = device(x, y, (zh + 1) % 4, zl, c), device(x, y, (zh + 3) % 4, zl, c)
    xn, xp = device((x + 1) % 4, y, zh, zl, c), device((x + 3) % 4, y, zh, zl, c)
    enter([device(x, my, zh, mz, mc) for my, mz, mc in mates] + [zn, zp, xn, xp])

    for arr, ref in enumerate((tok_ref, cot_ref)):
        for mz in range(2):
            packed32[...] = jnp.zeros_like(packed32)
            for my in range(4):
                col = (my * 2 + mz) * FEAT
                packed32[8 * (my // 2):8 * (my // 2) + ROWS, (my % 2) * FEAT:(my % 2 + 1) * FEAT] = (
                    ref[:, col:col + FEAT].astype(f32)
                )
            packed[mz, arr] = packed32[...].astype(bf)
    me = c * 8 + y * 2 + zl
    piece_copies = []
    for k, (my, mz, mc) in enumerate(mates):
        cp = remote(packed.at[mz, mc], pieces.at[me], ps.at[k], pr.at[k], device(x, my, zh, mz, mc))
        cp.start()
        piece_copies.append(cp)
    pieces[me] = packed[zl, c]

    weight_copies = []
    col_refs = (gate_ref, up_ref, pgate_ref, pup_ref)
    row_refs = (down_ref, pdown_ref)

    def cut(k, to):
        if k < 4:
            return (
                col_refs[k].at[:, pl.ds(pl.multiple_of(to * SUB, SUB), SUB)],
                wide.at[pl.ds(pl.multiple_of(y * FEAT, FEAT), FEAT), pl.ds(k * SUB, SUB)],
            )
        return (
            row_refs[k - 4].at[pl.ds(pl.multiple_of(to * SUB, SUB), SUB), :],
            tall.at[pl.ds((k - 4) * SUB, SUB), pl.ds(pl.multiple_of(y * FEAT, FEAT), FEAT)],
        )

    for k in range(6):
        for dy in (1, 3, 2):
            to = (y + dy) % 4
            src, dst = cut(k, to)
            cp = remote(src, dst, ws.at[dy - 1, k], wr.at[dy - 1, k], device(x, to, zh, zl, c))
            cp.start()
            weight_copies.append(cp)
        src, dst = cut(k, y)
        cp = pltpu.make_async_copy(src, dst, wl.at[k])
        cp.start()
        weight_copies.append(cp)

    sends = []

    def rows_of(dx, k):
        g = ((x + dx) % 4) * 4 + (zh + ZREL[k]) % 4
        return pl.ds(pl.multiple_of(g * GROUP, 16), GROUP)

    def where(dx, k, half=None):
        if half is None:
            return every.at[c, rows_of(dx, k), :]
        return every.at[c, rows_of(dx, k), pl.ds(half * HALF, HALF)]

    def go(src, dst, s, r, target):
        cp = remote(src, dst, s, r, target)
        cp.start()
        sends.append(cp)

    def arrive(dst, s, r):
        remote(dst, dst, s, r, sib).wait_recv()

    def share(dx, k):
        ref = where(dx, k)
        go(ref, ref, ss.at[dx * 4 + k], sr.at[dx * 4 + k], sib)

    def shared(dx):
        for k in range(4):
            arrive(every.at[1 - c, rows_of(dx, k), :], ss.at[dx * 4 + k], sr.at[dx * 4 + k])

    def along_x(k):
        ref = where(0, k)
        go(ref, ref, xs.at[0, k], xr.at[0, k], xn)
        go(ref, ref, xs.at[1, k], xr.at[1, k], xp)

    def pass_x(k):
        arrive(where(3, k), xs.at[0, k], xr.at[0, k])
        half = where(3, k, 0)
        go(half, half, xs.at[2, k], xr.at[2, k], xn)
        arrive(where(1, k), xs.at[1, k], xr.at[1, k])
        half = where(1, k, 1)
        go(half, half, xs.at[3, k], xr.at[3, k], xp)
        share(3, k)
        share(1, k)

    def end_x(k):
        arrive(where(2, k, 0), xs.at[2, k], xr.at[2, k])
        arrive(where(2, k, 1), xs.at[3, k], xr.at[3, k])
        share(2, k)

    def span(dx):
        return ((x + dx) % 4) * SPAN

    def partial(dx):
        rows = pl.ds(pl.multiple_of(span(dx), 16), SPAN)
        part[rows, 0:4 * SUB] = jnp.dot(every[0, rows, :], wide[...], preferred_element_type=f32).astype(bf)
        part[rows, 4 * SUB:] = lax.dot_general(
            every[1, rows, :], tall[...], (((1,), (1,)), ((), ())), preferred_element_type=f32
        ).astype(bf)
        theirs = pl.ds(pl.multiple_of(span(dx) + (1 - zl) * OWN, 16), OWN)
        go(part.at[theirs, :], far.at[dx], rs.at[dx], rr.at[dx], pair)

    def tangent(dx):
        arrive(far.at[dx], rs.at[dx], rr.at[dx])
        rows = pl.ds(pl.multiple_of(span(dx) + zl * OWN, 16), OWN)

        def total(n):
            cols = slice(n * SUB, (n + 1) * SUB)
            return part[rows, cols].astype(f32) + far[dx, :, cols].astype(f32)

        gate_pre, up_pre, gate_tan, up_tan, back, back_tan = (total(n) for n in range(6))
        logistic = 1.0 / (1.0 + jnp.exp(-gate_pre))
        activation = gate_pre * logistic
        first = logistic * (1.0 + gate_pre * (1.0 - logistic))
        second = logistic * (1.0 - logistic) * (2.0 + gate_pre * (1.0 - 2.0 * logistic))
        tans[rows, 0:SUB] = (
            back_tan * up_pre * first + back * up_tan * first + back * up_pre * second * gate_tan
        ).astype(bf)
        tans[rows, SUB:2 * SUB] = (back_tan * activation + back * first * gate_tan).astype(bf)
        tans[rows, 2 * SUB:] = (first * gate_tan * up_pre + activation * up_tan).astype(bf)
        go(tans.at[rows, :], tans.at[rows, :], ts.at[dx], tr.at[dx], pair)

    def tangent_there(dx):
        rows = pl.ds(pl.multiple_of(span(dx) + (1 - zl) * OWN, 16), OWN)
        arrive(tans.at[rows, :], ts.at[dx], tr.at[dx])

    g = x * 4 + zh
    for cp in piece_copies:
        cp.wait_recv()
    spread = pieces[...].reshape(256, 1024)
    for half in range(2):
        every[c, rows_of(0, 0), half * HALF:(half + 1) * HALF] = jnp.dot(
            pick_ref[half], spread, preferred_element_type=f32
        ).astype(bf)
    here = where(0, 0)
    go(here, here, zs.at[0], zr.at[0], zn)
    go(here, here, zs.at[1], zr.at[1], zp)
    along_x(0)
    share(0, 0)
    pass_x(0)
    arrive(where(0, 1), zs.at[0], zr.at[0])
    half = where(0, 1, 0)
    go(half, half, zs.at[2], zr.at[2], zn)
    arrive(where(0, 2), zs.at[1], zr.at[1])
    half = where(0, 2, 1)
    go(half, half, zs.at[3], zr.at[3], zp)
    along_x(1)
    along_x(2)
    share(0, 1)
    share(0, 2)
    end_x(0)
    arrive(where(0, 3, 0), zs.at[2], zr.at[2])
    arrive(where(0, 3, 1), zs.at[3], zr.at[3])
    along_x(3)
    share(0, 3)
    pass_x(1)
    pass_x(2)
    for cp in weight_copies:
        cp.wait()
    shared(0)
    partial(0)
    pass_x(3)
    end_x(1)
    end_x(2)
    shared(3)
    partial(3)
    shared(1)
    partial(1)
    tangent(0)
    end_x(3)
    tangent(3)
    shared(2)
    partial(2)
    tangent(1)
    tangent(2)
    for dx in (0, 3, 1, 2):
        tangent_there(dx)

    out_copies = []
    mine = pl.ds(pl.multiple_of(y * SUB, SUB), SUB)
    for dy in (2, 1, 3, 0):
        to = (y + dy) % 4
        feats = pl.ds(pl.multiple_of(to * FEAT, FEAT), FEAT)
        both = lax.dot_general(
            tans[:, 0:2 * SUB], every[0, :, feats], (((0,), (0,)), ((), ())), preferred_element_type=f32
        ) * (1.0 / TOKENS)
        back_wide[feats, :] = both.T.astype(bf)
        back_tall[:, feats] = (lax.dot_general(
            tans[:, 2 * SUB:], every[1, :, feats], (((0,), (0,)), ((), ())), preferred_element_type=f32
        ) * (1.0 / TOKENS)).astype(bf)
        pairs = (
            (back_wide.at[feats, pl.ds(0, SUB)], gate_out.at[:, mine]),
            (back_wide.at[feats, pl.ds(SUB, SUB)], up_out.at[:, mine]),
            (back_tall.at[:, feats], down_out.at[mine, :]),
        )
        for k, (src, dst) in enumerate(pairs):
            if dy:
                cp = remote(src, dst, os.at[dy - 1, k], orr.at[dy - 1, k], device(x, to, zh, zl, c))
            else:
                cp = pltpu.make_async_copy(src, dst, ol.at[k])
            cp.start()
            out_copies.append(cp)
    for cp in out_copies:
        cp.wait()
    for cp in piece_copies:
        cp.wait_send()
    for cp in sends:
        cp.wait_send()


def products_of(tokens, cotangent, gate, up, pgate, pup, down, pdown):
    pick = np.zeros((2, GROUP, 256), np.float32)
    for half in range(2):
        for row in range(GROUP):
            pick[half, row, 16 * (row // ROWS) + row % ROWS + 8 * half] = 1.0
    bf = jnp.bfloat16
    return pl.pallas_call(
        refresh_kernel,
        out_shape=(jax.ShapeDtypeStruct((FEAT, 4 * SUB), bf),) * 2 + (jax.ShapeDtypeStruct((4 * SUB, FEAT), bf),),
        in_specs=[VMEM] * 3 + [ANY] * 6,
        out_specs=(ANY, ANY, ANY),
        scratch_shapes=[
            pltpu.VMEM((16, 1024), jnp.float32),
            pltpu.VMEM((2, 2, 16, 1024), bf),
            pltpu.VMEM((16, 16, 1024), bf),
            pltpu.VMEM((2, TOKENS, WIDE), bf),
            pltpu.VMEM((WIDE, 4 * SUB), bf),
            pltpu.VMEM((2 * SUB, WIDE), bf),
            pltpu.VMEM((TOKENS, 6 * SUB), bf),
            pltpu.VMEM((NX, OWN, 6 * SUB), bf),
            pltpu.VMEM((TOKENS, 3 * SUB), bf),
            pltpu.VMEM((WIDE, 2 * SUB), bf),
            pltpu.VMEM((SUB, WIDE), bf),
            DMA((15,)), DMA((15,)),
            DMA((3, 6)), DMA((3, 6)), DMA((6,)),
            DMA((4,)), DMA((4,)),
            DMA((4, 4)), DMA((4, 4)),
            DMA((16,)), DMA((16,)),
            DMA((NX,)), DMA((NX,)), DMA((NX,)), DMA((NX,)),
            DMA((3, 3)), DMA((3, 3)), DMA((3,)),
        ],
        compiler_params=pltpu.CompilerParams(
            collective_id=0, has_side_effects=True, vmem_limit_bytes=60 << 20
        ),
    )(tokens, cotangent, jnp.asarray(pick, bf), gate, up, pgate, pup, down, pdown)


def sophia_update(hess_prev, probe, product, moment):
    new_hess = decay_rate * hess_prev + (1.0 - decay_rate) * probe.astype(jnp.float32) * product.astype(jnp.float32)
    ratio = moment.astype(jnp.float32) / jnp.maximum(curvature_scale * new_hess, floor_value)
    return new_hess, jnp.clip(ratio, -1.0, 1.0).astype(jnp.bfloat16)


def local(
    tokens, cotangent, gate_weight, up_weight, down_weight, probe_gate, probe_up, probe_down,
    hess_gate, hess_up, hess_down, moment_gate, moment_up, moment_down,
):
    products = products_of(
        tokens, cotangent, gate_weight, up_weight, probe_gate, probe_up, down_weight, probe_down
    )
    new_hess_gate, step_gate = sophia_update(hess_gate, probe_gate, products[0], moment_gate)
    new_hess_up, step_up = sophia_update(hess_up, probe_up, products[1], moment_up)
    new_hess_down, step_down = sophia_update(hess_down, probe_down, products[2], moment_down)
    return new_hess_gate, new_hess_up, new_hess_down, step_gate, step_up, step_down


def solution(mesh):
    cols, rows, split = P("tensor", "dp"), P("dp", "tensor"), P(("dp", "tensor"), None)
    per = (cols, cols, rows)
    return jax.shard_map(
        local, mesh=mesh,
        in_specs=(split, split) + per * 4,
        out_specs=per * 2,
        check_vma=False,
    )
```

time: 153 us -> 123 us (0.80)
  Pallas kernels: 129 us -> 116 us
  local copies, waits for them, and re-layouts: 10.2 us -> 0.04 us
  matrix products: 9.6 us -> 0 us
  other arithmetic: 3.66 us -> 5.32 us
    pallas_call x3 -> x1, Pallas kernels: 129 us -> 116 us  [products_of(): pl.pallas_call(refresh_kernel, out_shape=(jax.ShapeDtypeStruct((FEAT, 4 *...]
    unnamed x38 -> x16, local copies, waits for them, and re-layouts: 10.2 us -> 0.04 us
    dot_general x4 -> x0, matrix products: 9.6 us -> none  [the longest x1 4.21 us: local(): lax.dot_general(cots, tall, (((1,), (1,)), ((), ())), preferred_element_t...]
    convert_element_type x2, other arithmetic: 3.66 us -> 5.32 us  [sophia_update(): return (new_hess, jnp.clip(ratio, -1.0, 1.0).astype(jnp.bfloat16))]
where the time goes in v2:
time: 123 us
  Pallas kernels  116 us (94%)
  other arithmetic  5.32 us (4%)
    pallas_call x1, Pallas kernels, products_of(): pl.pallas_call(refresh_kernel, out_shape=(jax.ShapeDtypeStruct((FEAT, 4 *...  116 us
    convert_element_type x2, other arithmetic, sophia_update(): return (new_hess, jnp.clip(ratio, -1.0, 1.0).astype(jnp.bfloat16))  5.32 us

profile of v2, /device:TPU:1, one launch (start us, length us, event | category | flops | bytes accessed | tf_op | source)
XLA Modules:
  0.0 122.6 jit_solution(3374911191328850804)
XLA Ops:
  0.6 0.0 copy-start
  0.6 0.0 copy-start.1
  0.7 0.0 copy-start.5
  0.7 0.0 copy-start.4
  0.7 116.5 %shard_map.190 = (bf16[512,512]{1,0:T(8,128)(2,1)}, bf16[512,512]{1,0:T(8,128)(2,1)}, bf16[512,512]{1,0:T(8,128)(2,1)}) custom-call(bf16[5,4096]{1,0:T(8,128)(2,1)} %tok_ref.1, bf16[5,4096]{1,0:T(8,128)(2,1)} %cot_ref.1, bf16[2,80,256]{2,1,0:T(8,128)(2,1)} %constant.14.clone.pick_ref, bf16[512,512]{1,0:T(8,128)(2,1)} %gate_ref.1, bf16[512,512]{1,0:T(8,128)(2,1)} %up_ref.1, ...), custom_call_target="tpu_custom_call" | custom-call | tf_op jit(solution)/shard_map/pallas_call | solution.py:289
  117.1 0.0 copy-done
  117.1 0.0 copy-done.1
  117.2 0.0 copy-done.5
  117.2 0.0 copy-done.4
  117.2 0.0 copy-start.2
  117.2 0.0 copy-start.3
  117.2 0.0 copy-start.6
  117.2 0.0 copy-start.7
  117.2 3.8 %clamp_convert_fusion = (bf16[512,512]{1,0:T(8,128)(2,1)}, f32[512,512]{1,0:T(8,128)}, bf16[512,512]{1,0:T(8,128)(2,1)}, f32[512,512]{1,0:T(8,128)}) fusion(bf16[512,512]{1,0:T(8,128)(2,1)} %param.28, bf16[512,512]{1,0:T(8,128)(2,1)} %get-tuple-element.11, bf16[512,512]{1,0:T(8,128)(2,1)S(1)} %copy-done.1, f32[512,512]{1,0:T(8,128)S(1)} %copy-done.4, ...), kind=kLoop, calls=%fused_computation | loop fusion | flops 6291456 | bytes 8388608 | tf_op jit(solution)/shard_map/convert_element_type | solution.py:323
  121.0 0.0 copy-done.2
  121.0 0.0 copy-done.3
  121.0 0.0 copy-done.6
  121.0 0.0 copy-done.7
  121.0 1.6 %clamp_convert_fusion.2 = (bf16[512,512]{1,0:T(8,128)(2,1)}, f32[512,512]{1,0:T(8,128)}) fusion(bf16[512,512]{1,0:T(8,128)(2,1)S(1)} %copy-done.6, bf16[512,512]{1,0:T(8,128)(2,1)S(1)} %copy-done.7, bf16[512,512]{1,0:T(8,128)(2,1)S(1)} %copy-done.2, f32[512,512]{1,0:T(8,128)S(1)} %copy-done.3), kind=kLoop, calls=%fused_computation.2 | loop fusion | flops 3145728 | bytes 4194304 | tf_op jit(solution)/shard_map/convert_element_type | solution.py:323
Async XLA Ops:
  0.6 116.5 %copy-start = (bf16[512,512]{1,0:T(8,128)(2,1)S(1)}, bf16[512,512]{1,0:T(8,128)(2,1)}, u32[]{:S(2)}) copy-start(bf16[512,512]{1,0:T(8,128)(2,1)} %pup_ref.1) | copy-start | bytes 1572868
  0.6 116.5 %copy-start.1 = (bf16[512,512]{1,0:T(8,128)(2,1)S(1)}, bf16[512,512]{1,0:T(8,128)(2,1)}, u32[]{:S(2)}) copy-start(bf16[512,512]{1,0:T(8,128)(2,1)} %pdown_ref.1) | copy-start | bytes 1572868
  0.7 116.5 %copy-start.5 = (f32[512,512]{1,0:T(8,128)S(1)}, f32[512,512]{1,0:T(8,128)}, u32[]{:S(2)}) copy-start(f32[512,512]{1,0:T(8,128)} %param.24) | copy-start | bytes 3145732
  0.7 116.5 %copy-start.4 = (f32[512,512]{1,0:T(8,128)S(1)}, f32[512,512]{1,0:T(8,128)}, u32[]{:S(2)}) copy-start(f32[512,512]{1,0:T(8,128)} %param.25) | copy-start | bytes 3145732
  117.2 3.8 %copy-start.2 = (bf16[512,512]{1,0:T(8,128)(2,1)S(1)}, bf16[512,512]{1,0:T(8,128)(2,1)}, u32[]{:S(2)}) copy-start(bf16[512,512]{1,0:T(8,128)(2,1)} %pgate_ref.1) | copy-start | bytes 1572868
  117.2 3.8 %copy-start.3 = (f32[512,512]{1,0:T(8,128)S(1)}, f32[512,512]{1,0:T(8,128)}, u32[]{:S(2)}) copy-start(f32[512,512]{1,0:T(8,128)} %param.23) | copy-start | bytes 3145732
  117.2 3.8 %copy-start.6 = (bf16[512,512]{1,0:T(8,128)(2,1)S(1)}, bf16[512,512]{1,0:T(8,128)(2,1)}, u32[]{:S(2)}) copy-start(bf16[512,512]{1,0:T(8,128)(2,1)} %param.26) | copy-start | bytes 1572868
  117.2 3.8 %copy-start.7 = (bf16[512,512]{1,0:T(8,128)(2,1)S(1)}, bf16[512,512]{1,0:T(8,128)(2,1)}, u32[]{:S(2)}) copy-start(bf16[512,512]{1,0:T(8,128)(2,1)} %get-tuple-element.9) | copy-start | bytes 1572868

commit v3 on v2

v3 whole, which is shorter than its diff:
```python
import jax
import jax.numpy as jnp
import numpy as np
from jax import lax
from jax.experimental import pallas as pl
from jax.experimental.pallas import tpu as pltpu
from jax.sharding import PartitionSpec as P

decay_rate = 0.9
curvature_scale = 0.05
floor_value = 0.01

MESH = pl.DeviceIdType.MESH
ANY = pl.BlockSpec(memory_space=pl.ANY)
VMEM = pl.BlockSpec(memory_space=pltpu.VMEM)
DMA = pltpu.SemaphoreType.DMA

NX, NY, NZ = 4, 4, 4
ROWS = 5
GROUP = 80
FEAT = 512
WIDE = NY * FEAT
TOKENS = 1280
SUB = 128


def place():
    d = lax.axis_index("dp")
    t = lax.axis_index("tensor")
    return d // 8, t // 2, (d // 2) % 4, t % 2, d % 2


def device(x, y, zh, zl, c):
    return {"dp": x * 8 + zh * 2 + c, "tensor": y * 2 + zl}


def remote(src, dst, send, recv, target):
    return pltpu.make_async_remote_copy(
        src_ref=src, dst_ref=dst, send_sem=send, recv_sem=recv,
        device_id=target, device_id_type=MESH,
    )

LANE = WIDE // 2
HALF = LANE // 2
RUN = 768
SPAN = TOKENS // NZ
OWN = SPAN // 2
ZREL = (0, 3, 1, 2)
TOK, COT = 0, 1


def refresh_kernel(
    tok_ref, cot_ref, pick_ref, gate_ref, up_ref, pgate_ref, pup_ref, down_ref, pdown_ref,
    gate_out, up_out, down_out,
    packed32, packed, pieces, every, wide, tall, part_t, part_c, far_t, far_c, tan_h, tan_gu, back_wide, back_tall,
    ps, pr, ws, wr, wl, zs, zr, xs, xr, ss, sr, rs, rr, ts, tr, os, orr, ol,
):
    x, y, zh, zl, c = place()
    f32, bf = jnp.float32, jnp.bfloat16
    group = [(dc, dy, dz) for dc in range(2) for dy in range(4) for dz in range(2)][1:]
    mates = [((y + dy) % 4, zl ^ dz, c ^ dc) for dc, dy, dz in group]
    sib = device(x, y, zh, zl, 1 - c)
    pair = device(x, y, zh, 1 - zl, c)
    zn, zp = device(x, y, (zh + 1) % 4, zl, c), device(x, y, (zh + 3) % 4, zl, c)
    xn, xp = device((x + 1) % 4, y, zh, zl, c), device((x + 3) % 4, y, zh, zl, c)
    barrier = pltpu.get_barrier_semaphore()
    friends = [device(x, my, zh, mz, mc) for my, mz, mc in mates] + [zn, zp, xn, xp]
    for friend in friends:
        pl.semaphore_signal(barrier, inc=1, device_id=friend, device_id_type=MESH)

    packed32[...] = jnp.zeros_like(packed32)
    for mz in range(2):
        for mc in range(2):
            for n in range(8):
                ref = (tok_ref, cot_ref)[n // 4]
                col = ((2 * mc + n % 4 // 2) * 2 + mz) * FEAT + n % 2 * 256
                row, at = n // 3 * ROWS, n % 3 * 256
                packed32[row:row + ROWS, at:at + 256] = ref[:, col:col + 256].astype(f32)
            packed[mz, mc] = packed32[...].astype(bf)
    pl.semaphore_wait(barrier, len(friends))
    me = c * 8 + y * 2 + zl
    piece_copies = []
    for k, (my, mz, mc) in enumerate(mates):
        cp = remote(packed.at[mz, mc], pieces.at[me], ps.at[k], pr.at[k], device(x, my, zh, mz, mc))
        cp.start()
        piece_copies.append(cp)
    pieces[me] = packed[zl, c]

    weight_copies = []
    col_refs = (gate_ref, up_ref, pgate_ref, pup_ref)
    row_refs = (down_ref, pdown_ref)

    def cut(k, to):
        if k < 4:
            return (
                col_refs[k].at[:, pl.ds(pl.multiple_of(to * SUB, SUB), SUB)],
                wide.at[pl.ds(pl.multiple_of(y * FEAT, FEAT), FEAT), pl.ds(k * SUB, SUB)],
            )
        return (
            row_refs[k - 4].at[pl.ds(pl.multiple_of(to * SUB, SUB), SUB), :],
            tall.at[pl.ds((k - 4) * SUB, SUB), pl.ds(pl.multiple_of(y * FEAT, FEAT), FEAT)],
        )

    def lend(kinds):
        for k in kinds:
            for dy in (1, 3, 2):
                to = (y + dy) % 4
                src, dst = cut(k, to)
                cp = remote(src, dst, ws.at[dy - 1, k], wr.at[dy - 1, k], device(x, to, zh, zl, c))
                cp.start()
                weight_copies.append(cp)
            src, dst = cut(k, y)
            cp = pltpu.make_async_copy(src, dst, wl.at[k])
            cp.start()
            weight_copies.append(cp)

    sends = []

    def where(arr, dx, k, half=None):
        g = ((zh + ZREL[k]) % 4) * 4 + (x + dx) % 4
        rows = pl.ds(pl.multiple_of(g * GROUP, 16), GROUP)
        if half is None:
            return every.at[arr, rows, pl.ds(pl.multiple_of(c * LANE, LANE), LANE)]
        return every.at[arr, rows, pl.ds(pl.multiple_of(c * LANE + half * HALF, HALF), HALF)]

    def go(src, dst, s, r, target):
        cp = remote(src, dst, s, r, target)
        cp.start()
        sends.append(cp)

    def arrive(dst, s, r):
        remote(dst, dst, s, r, sib).wait_recv()

    def share(a, dx, k):
        ref = where(a, dx, k)
        go(ref, ref, ss.at[a, dx, k], sr.at[a, dx, k], sib)

    def shared(a, k):
        for dx in range(4):
            g = ((zh + ZREL[k]) % 4) * 4 + (x + dx) % 4
            rows = pl.ds(pl.multiple_of(g * GROUP, 16), GROUP)
            ref = every.at[a, rows, pl.ds(pl.multiple_of((1 - c) * LANE, LANE), LANE)]
            arrive(ref, ss.at[a, dx, k], sr.at[a, dx, k])

    def z_send(a, way, half):
        ref = where(a, 0, 0, half)
        cp = remote(ref, ref, zs.at[a, way, half], zr.at[a, way, half], (zn, zp)[way])
        cp.start()
        return cp

    def z_get(a, way, half):
        ref = where(a, 0, 1 + way, half)
        arrive(ref, zs.at[a, way, half], zr.at[a, way, half])
        if half == way:
            go(ref, ref, zs.at[a, way, 2], zr.at[a, way, 2], (zn, zp)[way])
        x_send(a, 1 + way, half)

    def z_end(a):
        for way in range(2):
            arrive(where(a, 0, 3, way), zs.at[a, way, 2], zr.at[a, way, 2])
            x_send(a, 3, way)
        share(a, 0, 3)

    def x_send(a, k, half):
        ref = where(a, 0, k, half)
        for way in (half, 1 - half):
            go(ref, ref, xs.at[a, way, k, half], xr.at[a, way, k, half], (xn, xp)[way])

    def x_get(a, way, k, half):
        ref = where(a, (3, 1)[way], k, half)
        arrive(ref, xs.at[a, way, k, half], xr.at[a, way, k, half])
        if half == way:
            go(ref, ref, xs.at[a, way, k, 2], xr.at[a, way, k, 2], (xn, xp)[way])

    def x_share(a, k):
        share(a, 3, k)
        share(a, 1, k)

    def x_end(a, k):
        for way in range(2):
            arrive(where(a, 2, k, way), xs.at[a, way, k, 2], xr.at[a, way, k, 2])
        share(a, 2, k)

    def span(k):
        return ((zh + ZREL[k]) % 4) * SPAN

    def rows_of(k):
        return pl.ds(pl.multiple_of(span(k), 16), SPAN)

    def near(k):
        return pl.ds(pl.multiple_of(span(k) + zl * OWN, 16), OWN)

    def away(k):
        return pl.ds(pl.multiple_of(span(k) + (1 - zl) * OWN, 16), OWN)

    def sum_t(k):
        shared(TOK, k)
        part_t[rows_of(k), :] = jnp.dot(every[TOK, rows_of(k), :], wide[...], preferred_element_type=f32).astype(bf)
        go(part_t.at[away(k), :], far_t.at[k], rs.at[0, k], rr.at[0, k], pair)

    def sum_c(k):
        shared(COT, k)
        part_c[rows_of(k), :] = lax.dot_general(
            every[COT, rows_of(k), :], tall[...], (((1,), (1,)), ((), ())), preferred_element_type=f32
        ).astype(bf)
        go(part_c.at[away(k), :], far_c.at[k], rs.at[1, k], rr.at[1, k], pair)

    def total_t(k, n):
        cols = slice(n * SUB, (n + 1) * SUB)
        return part_t[near(k), cols].astype(f32) + far_t[k, :, cols].astype(f32)

    def total_c(k, n):
        cols = slice(n * SUB, (n + 1) * SUB)
        return part_c[near(k), cols].astype(f32) + far_c[k, :, cols].astype(f32)

    def hidden(k):
        arrive(far_t.at[k], rs.at[0, k], rr.at[0, k])
        gate_pre, up_pre, gate_tan, up_tan = (total_t(k, n) for n in range(4))
        logistic = 1.0 / (1.0 + jnp.exp(-gate_pre))
        first = logistic * (1.0 + gate_pre * (1.0 - logistic))
        tan_h[near(k), :] = (first * gate_tan * up_pre + gate_pre * logistic * up_tan).astype(bf)
        ref = tan_h.at[near(k), :]
        go(ref, ref, ts.at[0, k], tr.at[0, k], pair)

    def tangent(k):
        arrive(far_c.at[k], rs.at[1, k], rr.at[1, k])
        gate_pre, up_pre, gate_tan, up_tan = (total_t(k, n) for n in range(4))
        back, back_tan = (total_c(k, n) for n in range(2))
        logistic = 1.0 / (1.0 + jnp.exp(-gate_pre))
        first = logistic * (1.0 + gate_pre * (1.0 - logistic))
        second = logistic * (1.0 - logistic) * (2.0 + gate_pre * (1.0 - 2.0 * logistic))
        tan_gu[near(k), 0:SUB] = (
            back_tan * up_pre * first + back * up_tan * first + back * up_pre * second * gate_tan
        ).astype(bf)
        tan_gu[near(k), SUB:] = (back_tan * gate_pre * logistic + back * first * gate_tan).astype(bf)
        ref = tan_gu.at[near(k), :]
        go(ref, ref, ts.at[1, k], tr.at[1, k], pair)

    def there(ref, n, k):
        ref = ref.at[away(k), :]
        arrive(ref, ts.at[n, k], tr.at[n, k])

    out_copies = []
    mine = pl.ds(pl.multiple_of(y * SUB, SUB), SUB)

    def give(dy, pairs):
        to = (y + dy) % 4
        for k, src, dst in pairs:
            if dy:
                cp = remote(src, dst, os.at[dy - 1, k], orr.at[dy - 1, k], device(x, to, zh, zl, c))
            else:
                cp = pltpu.make_async_copy(src, dst, ol.at[k])
            cp.start()
            out_copies.append(cp)

    def feats_of(dy):
        return pl.ds(pl.multiple_of(((y + dy) % 4) * FEAT, FEAT), FEAT)

    def product_down(dy):
        feats = feats_of(dy)
        back_tall[:, feats] = (lax.dot_general(
            tan_h[...], every[COT, :, feats], (((0,), (0,)), ((), ())), preferred_element_type=f32
        ) * (1.0 / TOKENS)).astype(bf)
        give(dy, [(2, back_tall.at[:, feats], down_out.at[mine, :])])

    def product_wide(dy):
        feats = feats_of(dy)
        both = lax.dot_general(
            tan_gu[...], every[TOK, :, feats], (((0,), (0,)), ((), ())), preferred_element_type=f32
        ) * (1.0 / TOKENS)
        back_wide[feats, :] = both.T.astype(bf)
        give(dy, [
            (0, back_wide.at[feats, pl.ds(0, SUB)], gate_out.at[:, mine]),
            (1, back_wide.at[feats, pl.ds(SUB, SUB)], up_out.at[:, mine]),
        ])

    for cp in piece_copies:
        cp.wait_recv()
    spread = pieces[...].reshape(256, RUN)
    block = jnp.concatenate([
        jnp.dot(pick_ref[n], spread[:, :min(RUN, WIDE - n * RUN)], preferred_element_type=f32).astype(bf)
        for n in range(3)
    ], axis=1)
    for arr in (TOK, COT):
        where(arr, 0, 0)[...] = block[:, arr * LANE:(arr + 1) * LANE]

    t_first = [z_send(TOK, 0, 0), z_send(TOK, 1, 1)]
    x_send(TOK, 0, 0)
    x_send(TOK, 0, 1)
    share(TOK, 0, 0)
    lend(range(6))
    for cp in t_first:
        cp.wait_send()
    sends.append(z_send(TOK, 0, 1))
    sends.append(z_send(TOK, 1, 0))
    x_get(TOK, 0, 0, 0)
    x_get(TOK, 1, 0, 1)
    z_get(TOK, 0, 0)
    z_get(TOK, 1, 1)
    x_get(TOK, 0, 0, 1)
    x_get(TOK, 1, 0, 0)
    x_share(TOK, 0)
    c_first = [z_send(COT, 0, 0), z_send(COT, 1, 1)]
    x_send(COT, 0, 0)
    x_send(COT, 0, 1)
    share(COT, 0, 0)
    z_get(TOK, 0, 1)
    z_get(TOK, 1, 0)
    share(TOK, 0, 1)
    share(TOK, 0, 2)
    x_end(TOK, 0)
    z_end(TOK)
    for cp in c_first:
        cp.wait_send()
    sends.append(z_send(COT, 0, 1))
    sends.append(z_send(COT, 1, 0))
    x_get(TOK, 0, 1, 0)
    x_get(TOK, 1, 2, 1)
    x_get(TOK, 1, 1, 1)
    x_get(TOK, 0, 2, 0)
    x_get(COT, 0, 0, 0)
    x_get(COT, 1, 0, 1)
    z_get(COT, 0, 0)
    z_get(COT, 1, 1)
    x_get(TOK, 1, 1, 0)
    x_get(TOK, 0, 2, 1)
    x_get(TOK, 0, 1, 1)
    x_get(TOK, 1, 2, 0)
    x_share(TOK, 1)
    x_share(TOK, 2)
    x_get(COT, 0, 0, 1)
    x_get(COT, 1, 0, 0)
    x_share(COT, 0)
    z_get(COT, 0, 1)
    z_get(COT, 1, 0)
    share(COT, 0, 1)
    share(COT, 0, 2)
    x_end(TOK, 1)
    x_end(TOK, 2)
    x_get(TOK, 0, 3, 0)
    x_get(TOK, 1, 3, 1)
    x_get(TOK, 0, 3, 1)
    x_get(TOK, 1, 3, 0)
    x_share(TOK, 3)
    z_end(COT)
    for cp in weight_copies[:16]:
        cp.wait()
    sum_t(0)
    x_end(COT, 0)
    x_get(COT, 0, 1, 0)
    x_get(COT, 1, 2, 1)
    sum_t(1)
    x_end(TOK, 3)
    sum_t(2)
    x_get(COT, 1, 1, 1)
    x_get(COT, 0, 2, 0)
    sum_t(3)
    x_get(COT, 1, 1, 0)
    x_get(COT, 0, 2, 1)
    x_get(COT, 0, 1, 1)
    x_get(COT, 1, 2, 0)
    x_share(COT, 1)
    x_share(COT, 2)
    hidden(0)
    for cp in weight_copies[16:]:
        cp.wait()
    sum_c(0)
    hidden(1)
    x_get(COT, 0, 3, 0)
    x_get(COT, 1, 3, 1)
    x_end(COT, 1)
    x_end(COT, 2)
    sum_c(1)
    hidden(2)
    x_get(COT, 0, 3, 1)
    x_get(COT, 1, 3, 0)
    x_share(COT, 3)
    sum_c(2)
    hidden(3)
    tangent(0)
    x_end(COT, 3)
    tangent(1)
    tangent(2)
    sum_c(3)
    for k in range(4):
        there(tan_h, 0, k)
    product_down(2)
    product_down(1)
    product_down(3)
    tangent(3)
    product_down(0)
    for k in range(4):
        there(tan_gu, 1, k)
    for dy in (2, 1, 3, 0):
        product_wide(dy)
    for cp in out_copies:
        cp.wait()
    for cp in piece_copies:
        cp.wait_send()
    for cp in sends:
        cp.wait_send()


def products_of(tokens, cotangent, gate, up, pgate, pup, down, pdown):
    pick = np.zeros((3, GROUP, 256), np.float32)
    for n in range(3):
        for row in range(GROUP):
            pick[n, row, 16 * (row // ROWS) + row % ROWS + ROWS * n] = 1.0
    bf = jnp.bfloat16
    return pl.pallas_call(
        refresh_kernel,
        out_shape=(jax.ShapeDtypeStruct((FEAT, 4 * SUB), bf),) * 2 + (jax.ShapeDtypeStruct((4 * SUB, FEAT), bf),),
        in_specs=[VMEM] * 3 + [ANY] * 6,
        out_specs=(ANY, ANY, ANY),
        scratch_shapes=[
            pltpu.VMEM((16, RUN), jnp.float32),
            pltpu.VMEM((2, 2, 16, RUN), bf),
            pltpu.VMEM((16, 16, RUN), bf),
            pltpu.VMEM((2, TOKENS, WIDE), bf),
            pltpu.VMEM((WIDE, 4 * SUB), bf),
            pltpu.VMEM((2 * SUB, WIDE), bf),
            pltpu.VMEM((TOKENS, 4 * SUB), bf),
            pltpu.VMEM((TOKENS, 2 * SUB), bf),
            pltpu.VMEM((NZ, OWN, 4 * SUB), bf),
            pltpu.VMEM((NZ, OWN, 2 * SUB), bf),
            pltpu.VMEM((TOKENS, SUB), bf),
            pltpu.VMEM((TOKENS, 2 * SUB), bf),
            pltpu.VMEM((WIDE, 2 * SUB), bf),
            pltpu.VMEM((SUB, WIDE), bf),
            DMA((15,)), DMA((15,)),
            DMA((3, 6)), DMA((3, 6)), DMA((6,)),
            DMA((2, 2, 3)), DMA((2, 2, 3)),
            DMA((2, 2, 4, 3)), DMA((2, 2, 4, 3)),
            DMA((2, 4, 4)), DMA((2, 4, 4)),
            DMA((2, NZ)), DMA((2, NZ)), DMA((2, NZ)), DMA((2, NZ)),
            DMA((3, 3)), DMA((3, 3)), DMA((3,)),
        ],
        compiler_params=pltpu.CompilerParams(
            collective_id=0, has_side_effects=True, vmem_limit_bytes=60 << 20
        ),
    )(tokens, cotangent, jnp.asarray(pick, bf), gate, up, pgate, pup, down, pdown)


def sophia_update(hess_prev, probe, product, moment):
    new_hess = decay_rate * hess_prev + (1.0 - decay_rate) * probe.astype(jnp.float32) * product.astype(jnp.float32)
    ratio = moment.astype(jnp.float32) / jnp.maximum(curvature_scale * new_hess, floor_value)
    return new_hess, jnp.clip(ratio, -1.0, 1.0).astype(jnp.bfloat16)


def local(
    tokens, cotangent, gate_weight, up_weight, down_weight, probe_gate, probe_up, probe_down,
    hess_gate, hess_up, hess_down, moment_gate, moment_up, moment_down,
):
    products = products_of(
        tokens, cotangent, gate_weight, up_weight, probe_gate, probe_up, down_weight, probe_down
    )
    new_hess_gate, step_gate = sophia_update(hess_gate, probe_gate, products[0], moment_gate)
    new_hess_up, step_up = sophia_update(hess_up, probe_up, products[1], moment_up)
    new_hess_down, step_down = sophia_update(hess_down, probe_down, products[2], moment_down)
    return new_hess_gate, new_hess_up, new_hess_down, step_gate, step_up, step_down


def solution(mesh):
    cols, rows, split = P("tensor", "dp"), P("dp", "tensor"), P(("dp", "tensor"), None)
    per = (cols, cols, rows)
    return jax.shard_map(
        local, mesh=mesh,
        in_specs=(split, split) + per * 4,
        out_specs=per * 2,
        check_vma=False,
    )
```

time: 123 us -> 106 us (0.86)
  Pallas kernels: 116 us -> 99.8 us
    pallas_call x1, Pallas kernels: 116 us -> 99.8 us  [products_of(): pl.pallas_call(refresh_kernel, out_shape=(jax.ShapeDtypeStruct((FEAT, 4 *...]
where the time goes in v3:
time: 106 us
  Pallas kernels  99.8 us (94%)
  other arithmetic  5.32 us (5%)
    pallas_call x1, Pallas kernels, products_of(): pl.pallas_call(refresh_kernel, out_shape=(jax.ShapeDtypeStruct((FEAT, 4 *...  99.8 us
    convert_element_type x2, other arithmetic, sophia_update(): return (new_hess, jnp.clip(ratio, -1.0, 1.0).astype(jnp.bfloat16))  5.32 us

profile of v3, /device:TPU:1, one launch (start us, length us, event | category | flops | bytes accessed | tf_op | source)
XLA Modules:
  0.0 105.9 jit_solution(3269076524709995957)
XLA Ops:
  0.6 0.0 copy-start
  0.6 0.0 copy-start.1
  0.7 0.0 copy-start.5
  0.7 0.0 copy-start.4
  0.7 99.8 %shard_map.190 = (bf16[512,512]{1,0:T(8,128)(2,1)}, bf16[512,512]{1,0:T(8,128)(2,1)}, bf16[512,512]{1,0:T(8,128)(2,1)}) custom-call(bf16[5,4096]{1,0:T(8,128)(2,1)} %tok_ref.1, bf16[5,4096]{1,0:T(8,128)(2,1)} %cot_ref.1, bf16[3,80,256]{2,1,0:T(8,128)(2,1)} %constant.14.clone.pick_ref, bf16[512,512]{1,0:T(8,128)(2,1)} %gate_ref.1, bf16[512,512]{1,0:T(8,128)(2,1)} %up_ref.1, ...), custom_call_target="tpu_custom_call" | custom-call | tf_op jit(solution)/shard_map/pallas_call | solution.py:410
  100.5 0.0 copy-done
  100.5 0.0 copy-done.1
  100.5 0.0 copy-done.5
  100.5 0.0 copy-done.4
  100.5 0.0 copy-start.2
  100.5 0.0 copy-start.3
  100.6 0.0 copy-start.6
  100.6 0.0 copy-start.7
  100.6 3.8 %clamp_convert_fusion = (bf16[512,512]{1,0:T(8,128)(2,1)}, f32[512,512]{1,0:T(8,128)}, bf16[512,512]{1,0:T(8,128)(2,1)}, f32[512,512]{1,0:T(8,128)}) fusion(bf16[512,512]{1,0:T(8,128)(2,1)} %param.28, bf16[512,512]{1,0:T(8,128)(2,1)} %get-tuple-element.11, bf16[512,512]{1,0:T(8,128)(2,1)S(1)} %copy-done.1, f32[512,512]{1,0:T(8,128)S(1)} %copy-done.4, ...), kind=kLoop, calls=%fused_computation | loop fusion | flops 6291456 | bytes 8388608 | tf_op jit(solution)/shard_map/convert_element_type | solution.py:447
  104.3 0.0 copy-done.2
  104.3 0.0 copy-done.3
  104.3 0.0 copy-done.6
  104.3 0.0 copy-done.7
  104.4 1.6 %clamp_convert_fusion.2 = (bf16[512,512]{1,0:T(8,128)(2,1)}, f32[512,512]{1,0:T(8,128)}) fusion(bf16[512,512]{1,0:T(8,128)(2,1)S(1)} %copy-done.6, bf16[512,512]{1,0:T(8,128)(2,1)S(1)} %copy-done.7, bf16[512,512]{1,0:T(8,128)(2,1)S(1)} %copy-done.2, f32[512,512]{1,0:T(8,128)S(1)} %copy-done.3), kind=kLoop, calls=%fused_computation.2 | loop fusion | flops 3145728 | bytes 4194304 | tf_op jit(solution)/shard_map/convert_element_type | solution.py:447
Async XLA Ops:
  0.6 99.9 %copy-start = (bf16[512,512]{1,0:T(8,128)(2,1)S(1)}, bf16[512,512]{1,0:T(8,128)(2,1)}, u32[]{:S(2)}) copy-start(bf16[512,512]{1,0:T(8,128)(2,1)} %pup_ref.1) | copy-start | bytes 1572868
  0.6 99.9 %copy-start.1 = (bf16[512,512]{1,0:T(8,128)(2,1)S(1)}, bf16[512,512]{1,0:T(8,128)(2,1)}, u32[]{:S(2)}) copy-start(bf16[512,512]{1,0:T(8,128)(2,1)} %pdown_ref.1) | copy-start | bytes 1572868
  0.7 99.9 %copy-start.5 = (f32[512,512]{1,0:T(8,128)S(1)}, f32[512,512]{1,0:T(8,128)}, u32[]{:S(2)}) copy-start(f32[512,512]{1,0:T(8,128)} %param.24) | copy-start | bytes 3145732
  0.7 99.9 %copy-start.4 = (f32[512,512]{1,0:T(8,128)S(1)}, f32[512,512]{1,0:T(8,128)}, u32[]{:S(2)}) copy-start(f32[512,512]{1,0:T(8,128)} %param.25) | copy-start | bytes 3145732
  100.5 3.8 %copy-start.2 = (bf16[512,512]{1,0:T(8,128)(2,1)S(1)}, bf16[512,512]{1,0:T(8,128)(2,1)}, u32[]{:S(2)}) copy-start(bf16[512,512]{1,0:T(8,128)(2,1)} %pgate_ref.1) | copy-start | bytes 1572868
  100.5 3.8 %copy-start.3 = (f32[512,512]{1,0:T(8,128)S(1)}, f32[512,512]{1,0:T(8,128)}, u32[]{:S(2)}) copy-start(f32[512,512]{1,0:T(8,128)} %param.23) | copy-start | bytes 3145732
  100.6 3.8 %copy-start.6 = (bf16[512,512]{1,0:T(8,128)(2,1)S(1)}, bf16[512,512]{1,0:T(8,128)(2,1)}, u32[]{:S(2)}) copy-start(bf16[512,512]{1,0:T(8,128)(2,1)} %param.26) | copy-start | bytes 1572868
  100.6 3.8 %copy-start.7 = (bf16[512,512]{1,0:T(8,128)(2,1)S(1)}, bf16[512,512]{1,0:T(8,128)(2,1)}, u32[]{:S(2)}) copy-start(bf16[512,512]{1,0:T(8,128)(2,1)} %get-tuple-element.9) | copy-start | bytes 1572868

commit v4 on v3

--- a/solution.py
+++ b/solution.py
@@ -42,7 +42,7 @@
 
 LANE = WIDE // 2
 HALF = LANE // 2
-RUN = 768
+RUN = 384
 SPAN = TOKENS // NZ
 OWN = SPAN // 2
 ZREL = (0, 3, 1, 2)
@@ -51,9 +51,11 @@
 
 def refresh_kernel(
     tok_ref, cot_ref, pick_ref, gate_ref, up_ref, pgate_ref, pup_ref, down_ref, pdown_ref,
-    gate_out, up_out, down_out,
+    hess_g, hess_u, hess_d, mom_g, mom_u, mom_d,
+    gate_out, up_out, down_out, hess_g_out, hess_u_out, hess_d_out, prb_g_out, prb_u_out, prb_d_out,
+    mom_g_out, mom_u_out, mom_d_out,
     packed32, packed, pieces, every, wide, tall, part_t, part_c, far_t, far_c, tan_h, tan_gu, back_wide, back_tall,
-    ps, pr, ws, wr, wl, zs, zr, xs, xr, ss, sr, rs, rr, ts, tr, os, orr, ol,
+    ps, pr, ws, wr, wl, zs, zr, xs, xr, ss, sr, rs, rr, ts, tr, os, orr, ol, near_sem,
 ):
     x, y, zh, zl, c = place()
     f32, bf = jnp.float32, jnp.bfloat16
@@ -63,28 +65,56 @@
     pair = device(x, y, zh, 1 - zl, c)
     zn, zp = device(x, y, (zh + 1) % 4, zl, c), device(x, y, (zh + 3) % 4, zl, c)
     xn, xp = device((x + 1) % 4, y, zh, zl, c), device((x + 3) % 4, y, zh, zl, c)
+    held = []
+    for k, (src, dst) in enumerate((
+        (hess_g, hess_g_out), (hess_u, hess_u_out), (hess_d, hess_d_out),
+        (pgate_ref, prb_g_out), (pup_ref, prb_u_out), (pdown_ref, prb_d_out),
+        (mom_g, mom_g_out), (mom_u, mom_u_out), (mom_d, mom_d_out),
+    )):
+        held.append(pltpu.make_async_copy(src, dst, near_sem.at[k]))
     barrier = pltpu.get_barrier_semaphore()
     friends = [device(x, my, zh, mz, mc) for my, mz, mc in mates] + [zn, zp, xn, xp]
     for friend in friends:
         pl.semaphore_signal(barrier, inc=1, device_id=friend, device_id_type=MESH)
 
     packed32[...] = jnp.zeros_like(packed32)
-    for mz in range(2):
-        for mc in range(2):
-            for n in range(8):
-                ref = (tok_ref, cot_ref)[n // 4]
-                col = ((2 * mc + n % 4 // 2) * 2 + mz) * FEAT + n % 2 * 256
-                row, at = n // 3 * ROWS, n % 3 * 256
-                packed32[row:row + ROWS, at:at + 256] = ref[:, col:col + 256].astype(f32)
-            packed[mz, mc] = packed32[...].astype(bf)
+
+    def pack(arr):
+        for mz in range(2):
+            for mc in range(2):
+                for n in range(8):
+                    col = ((2 * mc + n // 4) * 2 + mz) * FEAT + n % 4 * SUB
+                    row, at = n // 3 * ROWS, n % 3 * SUB
+                    packed32[row:row + ROWS, at:at + SUB] = (tok_ref, cot_ref)[arr][:, col:col + SUB].astype(f32)
+                packed[arr, mz, mc] = packed32[...].astype(bf)
+
+    me = c * 8 + y * 2 + zl
+    piece_copies = ([], [])
+
+    def scatter(arr):
+        for k, (my, mz, mc) in enumerate(mates):
+            cp = remote(
+                packed.at[arr, mz, mc], pieces.at[arr, me], ps.at[arr, k], pr.at[arr, k],
+                device(x, my, zh, mz, mc),
+            )
+            cp.start()
+            piece_copies[arr].append(cp)
+        pieces[arr, me] = packed[arr, zl, c]
+
+    def merge(arr):
+        for cp in piece_copies[arr]:
+            cp.wait_recv()
+        spread = pieces[arr].reshape(256, RUN)
+        where(arr, 0, 0)[...] = jnp.concatenate([
+            jnp.dot(pick_ref[n], spread[:, :min(RUN, LANE - n * RUN)], preferred_element_type=f32).astype(bf)
+            for n in range(3)
+        ], axis=1)
+
+    pack(TOK)
     pl.semaphore_wait(barrier, len(friends))
-    me = c * 8 + y * 2 + zl
-    piece_copies = []
-    for k, (my, mz, mc) in enumerate(mates):
-        cp = remote(packed.at[mz, mc], pieces.at[me], ps.at[k], pr.at[k], device(x, my, zh, mz, mc))
-        cp.start()
-        piece_copies.append(cp)
-    pieces[me] = packed[zl, c]
+    scatter(TOK)
+    pack(COT)
+    scatter(COT)
 
     weight_copies = []
     col_refs = (gate_ref, up_ref, pgate_ref, pup_ref)
@@ -274,52 +304,47 @@
             (1, back_wide.at[feats, pl.ds(SUB, SUB)], up_out.at[:, mine]),
         ])
 
-    for cp in piece_copies:
-        cp.wait_recv()
-    spread = pieces[...].reshape(256, RUN)
-    block = jnp.concatenate([
-        jnp.dot(pick_ref[n], spread[:, :min(RUN, WIDE - n * RUN)], preferred_element_type=f32).astype(bf)
-        for n in range(3)
-    ], axis=1)
-    for arr in (TOK, COT):
-        where(arr, 0, 0)[...] = block[:, arr * LANE:(arr + 1) * LANE]
-
+    lend(range(4))
+    for cp in held:
+        cp.start()
+    merge(TOK)
     t_first = [z_send(TOK, 0, 0), z_send(TOK, 1, 1)]
     x_send(TOK, 0, 0)
     x_send(TOK, 0, 1)
     share(TOK, 0, 0)
-    lend(range(6))
+    merge(COT)
     for cp in t_first:
         cp.wait_send()
     sends.append(z_send(TOK, 0, 1))
     sends.append(z_send(TOK, 1, 0))
+    x_send(COT, 0, 0)
+    x_send(COT, 0, 1)
+    share(COT, 0, 0)
     x_get(TOK, 0, 0, 0)
     x_get(TOK, 1, 0, 1)
     z_get(TOK, 0, 0)
     z_get(TOK, 1, 1)
+    c_first = [z_send(COT, 0, 0), z_send(COT, 1, 1)]
     x_get(TOK, 0, 0, 1)
     x_get(TOK, 1, 0, 0)
     x_share(TOK, 0)
-    c_first = [z_send(COT, 0, 0), z_send(COT, 1, 1)]
-    x_send(COT, 0, 0)
-    x_send(COT, 0, 1)
-    share(COT, 0, 0)
     z_get(TOK, 0, 1)
     z_get(TOK, 1, 0)
     share(TOK, 0, 1)
     share(TOK, 0, 2)
     x_end(TOK, 0)
     z_end(TOK)
+    lend((4, 5))
     for cp in c_first:
         cp.wait_send()
     sends.append(z_send(COT, 0, 1))
     sends.append(z_send(COT, 1, 0))
+    x_get(COT, 0, 0, 0)
+    x_get(COT, 1, 0, 1)
     x_get(TOK, 0, 1, 0)
     x_get(TOK, 1, 2, 1)
     x_get(TOK, 1, 1, 1)
     x_get(TOK, 0, 2, 0)
-    x_get(COT, 0, 0, 0)
-    x_get(COT, 1, 0, 1)
     z_get(COT, 0, 0)
     z_get(COT, 1, 1)
     x_get(TOK, 1, 1, 0)
@@ -335,23 +360,23 @@
     z_get(COT, 1, 0)
     share(COT, 0, 1)
     share(COT, 0, 2)
+    for cp in weight_copies[:16]:
+        cp.wait()
+    sum_t(0)
+    x_get(TOK, 0, 3, 0)
+    x_get(TOK, 1, 3, 1)
     x_end(TOK, 1)
     x_end(TOK, 2)
-    x_get(TOK, 0, 3, 0)
-    x_get(TOK, 1, 3, 1)
     x_get(TOK, 0, 3, 1)
     x_get(TOK, 1, 3, 0)
     x_share(TOK, 3)
     z_end(COT)
-    for cp in weight_copies[:16]:
-        cp.wait()
-    sum_t(0)
+    sum_t(1)
     x_end(COT, 0)
     x_get(COT, 0, 1, 0)
     x_get(COT, 1, 2, 1)
-    sum_t(1)
+    sum_t(2)
     x_end(TOK, 3)
-    sum_t(2)
     x_get(COT, 1, 1, 1)
     x_get(COT, 0, 2, 0)
     sum_t(3)
@@ -361,27 +386,25 @@
     x_get(COT, 1, 2, 0)
     x_share(COT, 1)
     x_share(COT, 2)
-    hidden(0)
     for cp in weight_copies[16:]:
         cp.wait()
     sum_c(0)
-    hidden(1)
     x_get(COT, 0, 3, 0)
     x_get(COT, 1, 3, 1)
     x_end(COT, 1)
     x_end(COT, 2)
     sum_c(1)
-    hidden(2)
+    sum_c(2)
     x_get(COT, 0, 3, 1)
     x_get(COT, 1, 3, 0)
     x_share(COT, 3)
-    sum_c(2)
-    hidden(3)
+    for k in range(4):
+        hidden(k)
+    x_end(COT, 3)
     tangent(0)
-    x_end(COT, 3)
+    sum_c(3)
     tangent(1)
     tangent(2)
-    sum_c(3)
     for k in range(4):
         there(tan_h, 0, k)
     product_down(2)
@@ -393,15 +416,18 @@
         there(tan_gu, 1, k)
     for dy in (2, 1, 3, 0):
         product_wide(dy)
+    for cp in held:
+        cp.wait()
     for cp in out_copies:
         cp.wait()
-    for cp in piece_copies:
-        cp.wait_send()
+    for arr in (TOK, COT):
+        for cp in piece_copies[arr]:
+            cp.wait_send()
     for cp in sends:
         cp.wait_send()
 
 
-def products_of(tokens, cotangent, gate, up, pgate, pup, down, pdown):
+def products_of(tokens, cotangent, gate, up, pgate, pup, down, pdown, *state):
     pick = np.zeros((3, GROUP, 256), np.float32)
     for n in range(3):
         for row in range(GROUP):
@@ -409,13 +435,13 @@
     bf = jnp.bfloat16
     return pl.pallas_call(
         refresh_kernel,
-        out_shape=(jax.ShapeDtypeStruct((FEAT, 4 * SUB), bf),) * 2 + (jax.ShapeDtypeStruct((4 * SUB, FEAT), bf),),
-        in_specs=[VMEM] * 3 + [ANY] * 6,
-        out_specs=(ANY, ANY, ANY),
+        out_shape=tuple(pltpu.VMEM((FEAT, FEAT), t) for t in (bf,) * 3 + (jnp.float32,) * 3 + (bf,) * 6),
+        in_specs=[VMEM] * 3 + [ANY] * 12,
+        out_specs=(VMEM,) * 12,
         scratch_shapes=[
             pltpu.VMEM((16, RUN), jnp.float32),
-            pltpu.VMEM((2, 2, 16, RUN), bf),
-            pltpu.VMEM((16, 16, RUN), bf),
+            pltpu.VMEM((2, 2, 2, 16, RUN), bf),
+            pltpu.VMEM((2, 16, 16, RUN), bf),
             pltpu.VMEM((2, TOKENS, WIDE), bf),
             pltpu.VMEM((WIDE, 4 * SUB), bf),
             pltpu.VMEM((2 * SUB, WIDE), bf),
@@ -427,18 +453,18 @@
             pltpu.VMEM((TOKENS, 2 * SUB), bf),
             pltpu.VMEM((WIDE, 2 * SUB), bf),
             pltpu.VMEM((SUB, WIDE), bf),
-            DMA((15,)), DMA((15,)),
+            DMA((2, 15)), DMA((2, 15)),
             DMA((3, 6)), DMA((3, 6)), DMA((6,)),
             DMA((2, 2, 3)), DMA((2, 2, 3)),
             DMA((2, 2, 4, 3)), DMA((2, 2, 4, 3)),
             DMA((2, 4, 4)), DMA((2, 4, 4)),
             DMA((2, NZ)), DMA((2, NZ)), DMA((2, NZ)), DMA((2, NZ)),
-            DMA((3, 3)), DMA((3, 3)), DMA((3,)),
+            DMA((3, 3)), DMA((3, 3)), DMA((3,)), DMA((9,)),
         ],
         compiler_params=pltpu.CompilerParams(
-            collective_id=0, has_side_effects=True, vmem_limit_bytes=60 << 20
+            collective_id=0, has_side_effects=True, vmem_limit_bytes=111 << 19
         ),
-    )(tokens, cotangent, jnp.asarray(pick, bf), gate, up, pgate, pup, down, pdown)
+    )(tokens, cotangent, jnp.asarray(pick, bf), gate, up, pgate, pup, down, pdown, *state)
 
 
 def sophia_update(hess_prev, probe, product, moment):
@@ -451,12 +477,14 @@
     tokens, cotangent, gate_weight, up_weight, down_weight, probe_gate, probe_up, probe_down,
     hess_gate, hess_up, hess_down, moment_gate, moment_up, moment_down,
 ):
-    products = products_of(
-        tokens, cotangent, gate_weight, up_weight, probe_gate, probe_up, down_weight, probe_down
+    held = products_of(
+        tokens, cotangent, gate_weight, up_weight, probe_gate, probe_up, down_weight, probe_down,
+        hess_gate, hess_up, hess_down, moment_gate, moment_up, moment_down,
     )
-    new_hess_gate, step_gate = sophia_update(hess_gate, probe_gate, products[0], moment_gate)
-    new_hess_up, step_up = sophia_update(hess_up, probe_up, products[1], moment_up)
-    new_hess_down, step_down = sophia_update(hess_down, probe_down, products[2], moment_down)
+    products, hess, probes, moments = held[:3], held[3:6], held[6:9], held[9:]
+    new_hess_gate, step_gate = sophia_update(hess[0], probes[0], products[0], moments[0])
+    new_hess_up, step_up = sophia_update(hess[1], probes[1], products[1], moments[1])
+    new_hess_down, step_down = sophia_update(hess[2], probes[2], products[2], moments[2])
     return new_hess_gate, new_hess_up, new_hess_down, step_gate, step_up, step_down
 
 

time: 106 us -> 100 us (0.943)
  Pallas kernels: 99.8 us -> 95.8 us
  other arithmetic: 5.32 us -> 3.65 us
    pallas_call x1, Pallas kernels: 99.8 us -> 95.8 us  [products_of(): pl.pallas_call(refresh_kernel, out_shape=tuple((pltpu.VMEM((FEAT, FEAT),...]
    convert_element_type x2, other arithmetic: 5.32 us -> 3.65 us  [sophia_update(): return (new_hess, jnp.clip(ratio, -1.0, 1.0).astype(jnp.bfloat16))]
where the time goes in v4:
time: 100 us
  Pallas kernels  95.8 us (96%)
  other arithmetic  3.65 us (4%)
    pallas_call x1, Pallas kernels, products_of(): pl.pallas_call(refresh_kernel, out_shape=tuple((pltpu.VMEM((FEAT, FEAT),...  95.8 us
    convert_element_type x2, other arithmetic, sophia_update(): return (new_hess, jnp.clip(ratio, -1.0, 1.0).astype(jnp.bfloat16))  3.65 us

profile of v4, /device:TPU:1, one launch (start us, length us, event | category | flops | bytes accessed | tf_op | source)
XLA Modules:
  0.0 100.1 jit_solution(9479960008419195294)
XLA Ops:
  0.6 95.8 %shard_map.190 = (bf16[512,512]{1,0:T(8,128)(2,1)S(1)}, bf16[512,512]{1,0:T(8,128)(2,1)S(1)}, bf16[512,512]{1,0:T(8,128)(2,1)S(1)}, f32[512,512]{1,0:T(8,128)S(1...) custom-call(bf16[5,4096]{1,0:T(8,128)(2,1)} %tok_ref.1, ...), custom_call_target="tpu_custom_call" | custom-call | tf_op jit(solution)/shard_map/pallas_call | solution.py:436
  96.4 1.6 %clamp_convert_fusion.2 = (bf16[512,512]{1,0:T(8,128)(2,1)}, f32[512,512]{1,0:T(8,128)}) fusion(bf16[512,512]{1,0:T(8,128)(2,1)S(1)} %get-tuple-element.27, bf16[512,512]{1,0:T(8,128)(2,1)S(1)} %get-tuple-element.20, bf16[512,512]{1,0:T(8,128)(2,1)S(1)} %get-tuple-element.19, f32[512,512]{1,0:T(8,128)S(1)} %get-tuple-element.18), kind=kLoop, calls=%fused_computation.2 | loop fusion | flops 3145728 | bytes 4194304 | tf_op jit(solution)/shard_map/convert_element_type | solution.py:473
  98.0 2.1 %clamp_convert_fusion = (bf16[512,512]{1,0:T(8,128)(2,1)}, f32[512,512]{1,0:T(8,128)}, bf16[512,512]{1,0:T(8,128)(2,1)}, f32[512,512]{1,0:T(8,128)}) fusion(bf16[512,512]{1,0:T(8,128)(2,1)S(1)} %get-tuple-element.29, bf16[512,512]{1,0:T(8,128)(2,1)S(1)} %get-tuple-element.26, bf16[512,512]{1,0:T(8,128)(2,1)S(1)} %get-tuple-element.25, ...), kind=kLoop, calls=%fused_computation | loop fusion | flops 6291456 | bytes 8388608 | tf_op jit(solution)/shard_map/convert_element_type | solution.py:473

commit v5 on v4

--- a/solution.py
+++ b/solution.py
@@ -391,6 +391,8 @@
     sum_c(0)
     x_get(COT, 0, 3, 0)
     x_get(COT, 1, 3, 1)
+    hidden(0)
+    hidden(1)
     x_end(COT, 1)
     x_end(COT, 2)
     sum_c(1)
@@ -398,10 +400,10 @@
     x_get(COT, 0, 3, 1)
     x_get(COT, 1, 3, 0)
     x_share(COT, 3)
-    for k in range(4):
-        hidden(k)
+    hidden(2)
+    hidden(3)
+    tangent(0)
     x_end(COT, 3)
-    tangent(0)
     sum_c(3)
     tangent(1)
     tangent(2)
@@ -416,15 +418,15 @@
         there(tan_gu, 1, k)
     for dy in (2, 1, 3, 0):
         product_wide(dy)
-    for cp in held:
-        cp.wait()
-    for cp in out_copies:
-        cp.wait()
     for arr in (TOK, COT):
         for cp in piece_copies[arr]:
             cp.wait_send()
     for cp in sends:
         cp.wait_send()
+    for cp in held:
+        cp.wait()
+    for cp in out_copies:
+        cp.wait()
 
 
 def products_of(tokens, cotangent, gate, up, pgate, pup, down, pdown, *state):

time: 100 us -> 99.5 us (level)
  no operation moved by 1% of the time
where the time goes in v5:
time: 99.5 us; the launch traced here: 99.4 us
  Pallas kernels  95.1 us (96%)
  other arithmetic  3.65 us (4%)
    pallas_call x1, Pallas kernels, products_of(): pl.pallas_call(refresh_kernel, out_shape=tuple((pltpu.VMEM((FEAT, FEAT),...  95.1 us
    convert_element_type x2, other arithmetic, sophia_update(): return (new_hess, jnp.clip(ratio, -1.0, 1.0).astype(jnp.bfloat16))  3.65 us

profile of v5, /device:TPU:1, one launch (start us, length us, event | category | flops | bytes accessed | tf_op | source)
XLA Modules:
  0.0 99.4 jit_solution(17360263032067602969)
XLA Ops:
  0.6 95.1 %shard_map.190 = (bf16[512,512]{1,0:T(8,128)(2,1)S(1)}, bf16[512,512]{1,0:T(8,128)(2,1)S(1)}, bf16[512,512]{1,0:T(8,128)(2,1)S(1)}, f32[512,512]{1,0:T(8,128)S(1...) custom-call(bf16[5,4096]{1,0:T(8,128)(2,1)} %tok_ref.1, ...), custom_call_target="tpu_custom_call" | custom-call | tf_op jit(solution)/shard_map/pallas_call | solution.py:438
  95.8 1.6 %clamp_convert_fusion.2 = (bf16[512,512]{1,0:T(8,128)(2,1)}, f32[512,512]{1,0:T(8,128)}) fusion(bf16[512,512]{1,0:T(8,128)(2,1)S(1)} %get-tuple-element.27, bf16[512,512]{1,0:T(8,128)(2,1)S(1)} %get-tuple-element.20, bf16[512,512]{1,0:T(8,128)(2,1)S(1)} %get-tuple-element.19, f32[512,512]{1,0:T(8,128)S(1)} %get-tuple-element.18), kind=kLoop, calls=%fused_computation.2 | loop fusion | flops 3145728 | bytes 4194304 | tf_op jit(solution)/shard_map/convert_element_type | solution.py:475
  97.3 2.1 %clamp_convert_fusion = (bf16[512,512]{1,0:T(8,128)(2,1)}, f32[512,512]{1,0:T(8,128)}, bf16[512,512]{1,0:T(8,128)(2,1)}, f32[512,512]{1,0:T(8,128)}) fusion(bf16[512,512]{1,0:T(8,128)(2,1)S(1)} %get-tuple-element.29, bf16[512,512]{1,0:T(8,128)(2,1)S(1)} %get-tuple-element.26, bf16[512,512]{1,0:T(8,128)(2,1)S(1)} %get-tuple-element.25, ...), kind=kLoop, calls=%fused_computation | loop fusion | flops 6291456 | bytes 8388608 | tf_op jit(solution)/shard_map/convert_element_type | solution.py:475
